TPU v7x, 32 devices: a whole 2x2x4 slice. The times are simulated.
32 devices in a mesh: batch: 8 (over y, x, core), tensor: 4 (over z).
Axes of the slice: x: 2, y: 2, z: 4, core: 2. Of those that a mesh axis runs over, the one named last changes fastest.
Arguments:
- inputs: bfloat16 [1024, 16, 768], P('tensor', 'batch'), may hold values from -6 to 6
- lengths: int32 [16], P('batch'), may hold values from 128 to 1024, as said below
- gain_one: bfloat16 [768], replicated, may hold values from 0.25 to 1.75
- qkv_weight: bfloat16 [3, 768, 768], P(None, None, 'tensor'), may hold values from -0.3125 to 0.3125
- out_weight: bfloat16 [768, 768], P('tensor'), may hold values from -2.5 to 2.5
- gain_two: bfloat16 [768], replicated, may hold values from 0.25 to 1.75
- up_projection_weight: bfloat16 [768, 3072], P(None, 'tensor'), may hold values from -0.21875 to 0.21875
- down_projection_weight: bfloat16 [3072, 768], P('tensor'), may hold values from -0.109375 to 0.109375
- pair_bias: float32 [1024, 512], replicated, may hold values from -3 to 3
- cotangent: bfloat16 [1024, 16, 768], P('tensor', 'batch'), may hold values from -6 to 6
Outputs:
- mixed: bfloat16 [1024, 16, 768], P('tensor', 'batch')
- grad_inputs: float32 [1024, 16, 768], P('tensor', 'batch')
- grad_gain_one: float32 [768], replicated
- grad_qkv: float32 [3, 768, 768], P(None, None, 'tensor')
- grad_out: float32 [768, 768], P('tensor')
- grad_gain_two: float32 [768], replicated
- up_weight_gradient: float32 [768, 3072], P(None, 'tensor')
- down_weight_gradient: float32 [3072, 768], P('tensor')
- grad_pair: float32 [1024, 512], replicated
Inputs may be any that keep to these rules, and one draw needn't show every extreme that they name: `lengths`: each length is a multiple of 128; among the 2 rows of each index of batch at least one, drawn from the seed, has length 1024.
All inputs are finite; a program needn't handle non-finite values.
Results may differ from a plain program's by a relative error of at most 0.017.
Values may be sent and summed in bfloat16 or wider, within the bound.
A program may use at most 192 MiB of HBM per device.

v0:
```python
import jax
import jax.numpy as jnp
from jax import lax
from jax.sharding import PartitionSpec as P


def layer_norm(values, gain):
    center = jnp.mean(values, axis=-1, keepdims=True)
    shifted = values - center
    spread = jnp.mean(shifted * shifted, axis=-1, keepdims=True)
    return shifted * lax.rsqrt(spread + 1e-05) * gain


def gelu_tanh(values):
    return jax.nn.gelu(values, approximate=True)


def band_full(pair_bias):
    length, doubled = pair_bias.shape
    half = doubled // 2
    padded = jnp.pad(pair_bias, ((0, 0), (0, length + 1)))
    flat = padded.reshape(-1)[: length * (length + doubled)]
    placed = flat.reshape(length, length + doubled)[:, half : half + length]
    offset = jnp.arange(length)[None, :] - jnp.arange(length)[:, None]
    inside = (offset >= -half) & (offset < half)
    return jnp.where(inside, jnp.exp(placed), 1.0)


def band_pick(square, doubled):
    length = square.shape[0]
    half = doubled // 2
    padded = jnp.pad(square, ((0, 0), (half, half)))
    flat = jnp.pad(padded.reshape(-1), (0, length))
    return flat.reshape(length, length + doubled + 1)[:, :doubled]


def per_device(
    inputs,
    lengths,
    gain_one,
    qkv_weight,
    out_weight,
    gain_two,
    up_projection_weight,
    down_projection_weight,
    pair_bias,
    cotangent,
):
    channels = qkv_weight.shape[2]
    inputs_float = inputs.astype(jnp.float32)
    normed_one, norm_one_back = jax.vjp(layer_norm, inputs_float, gain_one.astype(jnp.float32))
    full_one = lax.all_gather(normed_one.astype(jnp.bfloat16), "tensor", axis=0, tiled=True)
    length = full_one.shape[0]
    projected = jnp.einsum(
        "trd,kdc->ktrc", full_one, qkv_weight, preferred_element_type=jnp.float32
    )
    queries = projected[0]
    key_part = projected[1]
    values = projected[2]
    positions = jnp.arange(length)
    keep_mask = (positions[:, None] < lengths[None, :]).astype(jnp.float32)
    weights_exp = keep_mask[:, :, None] * jnp.exp(key_part)
    pairs = jnp.concatenate([weights_exp * values, weights_exp], axis=-1).astype(jnp.bfloat16)
    band_float = band_full(pair_bias)
    band_low = band_float.astype(jnp.bfloat16)
    sums = jnp.einsum("ts,src->trc", band_low, pairs, preferred_element_type=jnp.float32)
    numer = sums[..., :channels]
    denom = sums[..., channels:]
    gates = jax.nn.sigmoid(queries)
    ratio = numer / denom
    mixer = (gates * ratio).astype(jnp.bfloat16)
    selected_rows = mixer
    branch = lax.psum_scatter(
        jnp.einsum(
            "trc,cd->trd", selected_rows, out_weight, preferred_element_type=jnp.float32
        ).astype(jnp.bfloat16),
        "tensor",
        scatter_dimension=0,
        tiled=True,
    ).astype(jnp.float32)
    middle = inputs_float + branch
    second_normalized, norm_two_back = jax.vjp(layer_norm, middle, gain_two.astype(jnp.float32))
    second_full_block = lax.all_gather(
        second_normalized.astype(jnp.bfloat16), "tensor", axis=0, tiled=True
    )
    hidden_state = jnp.einsum(
        "eaj,jy->eay", second_full_block, up_projection_weight, preferred_element_type=jnp.float32
    )
    active_float, gelu_back = jax.vjp(gelu_tanh, hidden_state)
    active_rows = active_float.astype(jnp.bfloat16)
    selected_rows = active_rows
    second_branch = lax.psum_scatter(
        jnp.einsum(
            "qoa,aj->qoj", selected_rows, down_projection_weight, preferred_element_type=jnp.float32
        ).astype(jnp.bfloat16),
        "tensor",
        scatter_dimension=0,
        tiled=True,
    ).astype(jnp.float32)
    mixed = (middle + second_branch).astype(jnp.bfloat16)
    cotangent_block = lax.all_gather(cotangent, "tensor", axis=0, tiled=True)
    down_weight_gradient = jnp.einsum(
        "mop,moq->pq", active_rows, cotangent_block, preferred_element_type=jnp.float32
    )
    grad_active = jnp.einsum(
        "yqg,zg->yqz", cotangent_block, down_projection_weight, preferred_element_type=jnp.float32
    )
    hidden_gradient = gelu_back(grad_active)[0].astype(jnp.bfloat16)
    up_weight_gradient = jnp.einsum(
        "vyz,vym->zm", second_full_block, hidden_gradient, preferred_element_type=jnp.float32
    )
    selected_rows = hidden_gradient
    grad_normed_two = lax.psum_scatter(
        jnp.einsum(
            "mwv,gv->mwg", selected_rows, up_projection_weight, preferred_element_type=jnp.float32
        ).astype(jnp.bfloat16),
        "tensor",
        scatter_dimension=0,
        tiled=True,
    ).astype(jnp.float32)
    grad_middle_norm, grad_gain_two = norm_two_back(grad_normed_two)
    grad_middle = cotangent.astype(jnp.float32) + grad_middle_norm
    res_full = lax.all_gather(grad_middle.astype(jnp.bfloat16), "tensor", axis=0, tiled=True)
    grad_out = jnp.einsum("trc,trd->cd", mixer, res_full, preferred_element_type=jnp.float32)
    grad_mixer = jnp.einsum("trd,cd->trc", res_full, out_weight, preferred_element_type=jnp.float32)
    grad_queries = (grad_mixer * ratio * gates * (1.0 - gates)).astype(jnp.bfloat16)
    scaled = grad_mixer * gates / denom
    grad_sums = jnp.concatenate([scaled, -scaled * ratio], axis=-1).astype(jnp.bfloat16)
    grad_band = jnp.einsum("trc,src->ts", grad_sums, pairs, preferred_element_type=jnp.float32)
    grad_pairs = jnp.einsum("ts,trc->src", band_low, grad_sums, preferred_element_type=jnp.float32)
    grad_numer = grad_pairs[..., :channels]
    grad_denom = grad_pairs[..., channels:]
    grad_keys = ((grad_numer * values + grad_denom) * weights_exp).astype(jnp.bfloat16)
    grad_values = (grad_numer * weights_exp).astype(jnp.bfloat16)
    grad_proj = jnp.stack([grad_queries, grad_keys, grad_values])
    grad_qkv = jnp.einsum("trd,ktrc->kdc", full_one, grad_proj, preferred_element_type=jnp.float32)
    selected_rows = grad_proj
    grad_normed_one = lax.psum_scatter(
        jnp.einsum(
            "ktrc,kdc->trd", selected_rows, qkv_weight, preferred_element_type=jnp.float32
        ).astype(jnp.bfloat16),
        "tensor",
        scatter_dimension=0,
        tiled=True,
    ).astype(jnp.float32)
    grad_input_norm, grad_gain_one = norm_one_back(grad_normed_one)
    grad_inputs = grad_middle + grad_input_norm
    grad_pair = band_pick(grad_band * band_float, pair_bias.shape[1])
    grad_gain_one, grad_gain_two, grad_pair = lax.psum(
        (grad_gain_one, grad_gain_two, grad_pair), ("batch", "tensor")
    )
    grad_qkv, grad_out, up_weight_gradient, down_weight_gradient = lax.psum(
        (grad_qkv, grad_out, up_weight_gradient, down_weight_gradient), "batch"
    )
    return (
        mixed,
        grad_inputs,
        grad_gain_one,
        grad_qkv,
        grad_out,
        grad_gain_two,
        up_weight_gradient,
        down_weight_gradient,
        grad_pair,
    )


def solution(mesh):
    return jax.shard_map(
        per_device,
        mesh=mesh,
        in_specs=(
            P("tensor", "batch", None),
            P("batch"),
            P(),
            P(None, None, "tensor"),
            P("tensor", None),
            P(),
            P(None, "tensor"),
            P("tensor", None),
            P(),
            P("tensor", "batch", None),
        ),
        out_specs=(
            P("tensor", "batch", None),
            P("tensor", "batch", None),
            P(),
            P(None, None, "tensor"),
            P("tensor", None),
            P(),
            P(None, "tensor"),
            P("tensor", None),
            P(),
        ),
        check_vma=False,
    )
```

profile of v0, /device:TPU:0, one launch (start us, length us, event | category | flops | bytes accessed | tf_op | source)
XLA Modules:
  0.0 835.3 jit_solution(13044459435409013272)
XLA Ops:
  7.3 1.4 convert_reduce_fusion
  8.7 1.5 fusion.32
  10.2 0.7 convert_element_type.85
  10.9 1.2 fusion.28
  12.2 4.8 pad.12
  17.0 10.1 %reshape.112 = f32[1573888]{0:T(1024)} reshape(f32[1024,1537]{1,0:T(8,128)} %pad.12) | data formatting | bytes 12591104 | tf_op jit(solution)/shard_map/reshape | solution.py:22
  27.1 4.7 slice.41
  31.8 7.3 reshape.113
  39.2 39.3 %all-gather.5.cloned.1.call-done = bf16[1024,2,768]{2,0,1:T(8,128)(2,1)} async-done(((bf16[256,2,768]{2,0,1:T(8,128)(2,1)}), bf16[1024,2,768]{2,0,1:T(8,128)(2,1)}) %all-gather.5.cloned.1.call-update) | async-done | bytes 3145744 | tf_op jit(solution)/shard_map/all_gather | solution.py:52
  78.4 4.3 fusion.19
  83.2 1.8 fusion.55
  85.3 0.6 multiply_convert_fusion.5
  86.0 1.1 copy-done.5
  87.0 2.8 convolution_convert_fusion
  89.9 0.6 copy-done.38
  90.5 58.4 %reduce-scatter.5.cloned.1.call-done = bf16[256,2,768]{2,0,1:T(8,128)(2,1)} async-done(((bf16[1024,2,768]{2,0,1:T(8,128)(2,1)}), bf16[256,2,768]{2,0,1:T(8,128)(2,1)}) %reduce-scatter.5.cloned.1.call-update) | async-done | bytes 786448 | tf_op jit(solution)/shard_map/reduce_scatter | solution.py:73
  148.9 1.4 fusion.48
  150.7 0.6 copy-done.36
  151.3 0.6 copy-done.30
  151.9 1.2 multiply_convert_fusion.4
  153.6 2.1 copy.34
  155.8 61.0 %all-gather.7.cloned.1.call-done = bf16[1024,2,768]{2,0,1:T(8,128)(2,1)} async-done(((bf16[256,2,768]{2,0,1:T(8,128)(2,1)}), bf16[1024,2,768]{2,0,1:T(8,128)(2,1)}) %all-gather.7.cloned.1.call-update) | async-done | bytes 3145744 | tf_op jit(solution)/shard_map/all_gather | solution.py:83
  216.8 7.1 fusion.52
  223.9 57.0 %all-gather.9.cloned.1.call-done = bf16[1024,2,768]{2,0,1:T(8,128)(2,1)} async-done(((bf16[256,2,768]{2,0,1:T(8,128)(2,1)}), bf16[1024,2,768]{2,0,1:T(8,128)(2,1)}) %all-gather.9.cloned.1.call-update) | async-done | bytes 3145744 | tf_op jit(solution)/shard_map/all_gather | solution.py:101
  280.9 8.3 fusion.6
  289.3 1.6 copy-done.42
  290.9 4.0 convolution_convert_fusion.1
  295.0 59.0 %reduce-scatter.9.cloned.1.call-done = bf16[256,2,768]{2,0,1:T(8,128)(2,1)} async-done(((bf16[1024,2,768]{2,0,1:T(8,128)(2,1)}), bf16[256,2,768]{2,0,1:T(8,128)(2,1)}) %reduce-scatter.9.cloned.1.call-update) | async-done | bytes 786448 | tf_op jit(solution)/shard_map/reduce_scatter | solution.py:113
  354.1 1.7 fusion.29
  355.8 1.0 fusion.30
  356.9 1.5 fusion.57
  358.6 63.4 %all-gather.11.cloned.1.call-done = bf16[1024,2,768]{2,0,1:T(8,128)(2,1)} async-done(((bf16[256,2,768]{2,0,1:T(8,128)(2,1)}), bf16[1024,2,768]{2,0,1:T(8,128)(2,1)}) %all-gather.11.cloned.1.call-update) | async-done | bytes 3145744 | tf_op jit(solution)/shard_map/all_gather | solution.py:123
  422.1 4.9 fusion.83
  428.5 4.7 fusion.54
  433.2 0.8 fusion.62
  434.1 0.8 copy-done.19
  435.2 4.1 bitcast_convert_fusion
  439.3 8.6 %convolution_convert_fusion.2 = bf16[1024,2,768]{2,0,1:T(8,128)(2,1)} fusion(bf16[768,768]{1,0:T(8,128)(2,1)} %param.17, f32[1024,2,768]{2,0,1:T(8,128)} %fusion.52), kind=kOutput, calls=%fused_computation.35 | convolution fusion | flops 2431647744 | bytes 10616832 | tf_op jit(solution)/shard_map/qoa,aj->qoj/dot_general | solution.py:93
  448.2 8.5 %convolution_bitcast_fusion = f32[768,768]{1,0:T(8,128)} fusion(bf16[1024,2,768]{2,0,1:T(8,128)(2,1)} %all-gather.9.cloned.1.call-done, f32[1024,2,768]{2,0,1:T(8,128)} %fusion.52), kind=kOutput, calls=%fused_computation.46 | convolution fusion | flops 2430074880 | bytes 11796480 | tf_op jit(solution)/shard_map/mop,moq->pq/dot_general | solution.py:102
  456.7 4.2 bitcast_multiply_fusion
  460.9 3.3 pad.13
  464.2 7.0 reshape.114
  471.2 4.8 pad.14
  476.1 10.4 %reshape.115 = f32[1024,1537]{1,0:T(8,128)} reshape(f32[1573888]{0:T(1024)} %pad.14) | data formatting | bytes 12591104 | tf_op jit(solution)/shard_map/reshape | solution.py:34
  486.4 3.1 slice.49
  489.9 7.1 convolution_bitcast_fusion.1
  496.9 1.7 convolution_bitcast_fusion.2
  498.6 3.2 fusion.44
  501.9 1.7 fusion.33
  503.6 0.9 fusion.31
  504.6 56.4 %reduce-scatter.7.cloned.1.call-done = bf16[256,2,768]{2,0,1:T(8,128)(2,1)} async-done(((bf16[1024,2,768]{2,0,1:T(8,128)(2,1)}), bf16[256,2,768]{2,0,1:T(8,128)(2,1)}) %reduce-scatter.7.cloned.1.call-update) | async-done | bytes 786448 | tf_op jit(solution)/shard_map/reduce_scatter | solution.py:92
  561.0 2.5 add_add_fusion.2
  563.5 2.4 copy.42
  565.8 1.7 copy.41
  567.5 40.5 %all-reduce.3 = (f32[768]{0:T(1024)}, f32[768]{0:T(1024)}) all-reduce(f32[768]{0:T(1024)S(1)} %get-tuple-element.29, f32[768]{0:T(1024)S(1)} %get-tuple-element.27), channel_id=1, replica_groups=mesh['batch'=8,'tensor'=4] {'batch','tensor'}, use_global_device_ids=true, to_apply=%region_13.14 | all-reduce | flops 1536 | bytes 12288 | tf_op jit(solution)/shard_map/psum | solution.py:149
  608.0 93.0 %all-reduce.8.cloned.1.call-done = f32[1024,512]{1,0:T(8,128)} async-done(((f32[1024,512]{1,0:T(8,128)}), f32[1024,512]{1,0:T(8,128)}) %all-reduce.8.cloned.1.call-update) | async-done | bytes 2097168 | tf_op jit(solution)/shard_map/psum | solution.py:149
  701.0 117.0 %all-reduce.10.cloned.1.call-done = (f32[3,768,192]{1,2,0:T(8,128)}, f32[192,768]{1,0:T(8,128)}, f32[768,768]{1,0:T(8,128)}, f32[768,768]{1,0:T(8,128)}) async-done(((f32[3,768,192]{1,2,0:T(8,128)}, f32[192,768]{1,0:T(8,128)}, f32[768,768]{1,0:T(8,128)}, f32[768,768]{1,0:T(8,128)}), (f32[3,768,192]{1,2,0:T(8,128)}, f32[192,768]{1,0:T(8,128)}, f32[768,768]{1,0:T(8,128)}, ...) | async-done | bytes 7077904 | tf_op jit(solution)/shard_map/psum | solution.py:152
  818.0 2.9 copy.75
  820.9 0.8 copy.76
  821.8 1.4 copy.77
  823.2 1.1 copy-done.12
  824.3 1.4 copy.78
  825.7 1.0 copy-done.14
  826.7 1.3 copy.79
  (125 shorter events, 4.9 us)
Async XLA Ops:
  7.2 209.6 %copy-start = (bf16[768,768]{1,0:T(8,128)(2,1)S(1)}, bf16[768,768]{1,0:T(8,128)(2,1)}, u32[]{:S(2)}) copy-start(bf16[768,768]{1,0:T(8,128)(2,1)} %param.16) | copy-start | bytes 3538948
  7.2 3.7 copy-start.2
  7.2 71.2 %all-gather.5.cloned.1.call-start = ((), (), s32[]{:S(2)}) async-start(), calls=%async_computation.4 | async-start | bytes 3932160 | tf_op jit(solution)/shard_map/all_gather | solution.py:52
  10.2 6.8 copy-start.34
  10.2 6.8 copy-start.32
  12.1 136.8 %reduce-scatter.5.cloned.1.call-start = ((), (), s32[]{:S(2)}) async-start(), calls=%async_computation.5 | async-start | bytes 3932160 | tf_op jit(solution)/shard_map/reduce_scatter | solution.py:73
  31.8 7.3 copy-start.39
  39.2 43.6 %copy-start.28 = (f32[1024,2]{0,1:T(2,128)}, f32[1024,2]{0,1:T(2,128)S(1)}, u32[]{:S(2)}) copy-start(f32[1024,2]{0,1:T(2,128)S(1)} %compare_convert_fusion) | copy-start | bytes 24580
  78.4 4.7 copy-start.10
  82.7 2.3 copy-start.4
  83.2 2.0 copy-start.15
  83.2 2.2 copy-start.17
  85.3 1.7 copy-start.5
  85.3 1.7 copy-start.26
  89.8 0.7 copy-start.38
  89.8 127.0 %all-gather.7.cloned.1.call-start = ((), (), s32[]{:S(2)}) async-start(), calls=%async_computation.6 | async-start | bytes 3932160 | tf_op jit(solution)/shard_map/all_gather | solution.py:83
  148.9 1.5 copy-start.3
  150.7 0.6 copy-start.36
  151.3 0.6 copy-start.30
  153.1 127.8 %all-gather.9.cloned.1.call-start = ((), (), s32[]{:S(2)}) async-start(), calls=%async_computation.8 | async-start | bytes 3932160 | tf_op jit(solution)/shard_map/all_gather | solution.py:101
  155.7 198.3 %reduce-scatter.9.cloned.1.call-start = ((), (), s32[]{:S(2)}) async-start(), calls=%async_computation.9 | async-start | bytes 3932160 | tf_op jit(solution)/shard_map/reduce_scatter | solution.py:113
  289.3 1.6 copy-start.42
  295.0 60.8 %copy-start.37 = (f32[256,2]{0,1:T(2,128)S(1)}, f32[256,2]{0,1:T(2,128)}, u32[]{:S(2)}) copy-start(f32[256,2]{0,1:T(2,128)} %copy-done.36) | copy-start | bytes 6148
  295.0 60.8 %copy-start.31 = (f32[256,2]{0,1:T(2,128)S(1)}, f32[256,2]{0,1:T(2,128)}, u32[]{:S(2)}) copy-start(f32[256,2]{0,1:T(2,128)} %copy-done.30) | copy-start | bytes 6148
  295.0 127.1 %all-gather.11.cloned.1.call-start = ((), (), s32[]{:S(2)}) async-start(), calls=%async_computation.10 | async-start | bytes 3932160 | tf_op jit(solution)/shard_map/all_gather | solution.py:123
  354.1 1.7 copy-start.7
  355.8 1.1 copy-start.9
  356.9 65.2 %copy-start.27 = (bf16[192,768]{1,0:T(8,128)(2,1)S(1)}, bf16[192,768]{1,0:T(8,128)(2,1)}, u32[]{:S(2)}) copy-start(bf16[192,768]{1,0:T(8,128)(2,1)} %param.14) | copy-start | bytes 884740
  358.4 143.4 %reduce-scatter.11.cloned.1.call-start = ((), (), s32[]{:S(2)}) async-start(), calls=%async_computation.11 | async-start | bytes 3932160 | tf_op jit(solution)/shard_map/reduce_scatter | solution.py:138
  422.1 4.9 copy-start.6
  427.0 1.0 copy-start.45
  427.0 7.1 copy-start.43
  427.0 6.1 slice-start
  427.6 0.9 copy-start.23
  428.4 4.7 slice-start.1
  428.4 4.7 copy-start.29
  433.2 2.0 copy-start.41
  434.0 0.9 copy-start.19
  434.0 1.1 copy-start.21
  439.3 121.7 %reduce-scatter.7.cloned.1.call-start = ((), (), s32[]{:S(2)}) async-start(), calls=%async_computation.7 | async-start | bytes 3932160 | tf_op jit(solution)/shard_map/reduce_scatter | solution.py:92
  447.9 253.1 %all-reduce.8.cloned.1.call-start = ((), (), s32[]{:S(2)}) async-start(), calls=%async_computation.12 | async-start | bytes 4194304 | tf_op jit(solution)/shard_map/psum | solution.py:149
  448.2 8.5 %copy-start.16 = (bf16[1024,2,192]{0,2,1:T(8,128)(2,1)S(1)}, bf16[1024,2,192]{0,2,1:T(8,128)(2,1)}, u32[]{:S(2)}) copy-start(bf16[1024,2,192]{0,2,1:T(8,128)(2,1)} %copy-done.15) | copy-start | bytes 2359300
  448.2 8.5 %copy-start.18 = (bf16[1024,2,192]{0,2,1:T(8,128)(2,1)S(1)}, bf16[1024,2,192]{0,2,1:T(8,128)(2,1)}, u32[]{:S(2)}) copy-start(bf16[1024,2,192]{0,2,1:T(8,128)(2,1)} %copy-done.17) | copy-start | bytes 2359300
  448.2 8.5 %copy-start.24 = (bf16[1024,2,192]{0,2,1:T(8,128)(2,1)S(1)}, bf16[1024,2,192]{0,2,1:T(8,128)(2,1)}, u32[]{:S(2)}) copy-start(bf16[1024,2,192]{0,2,1:T(8,128)(2,1)} %copy-done.23) | copy-start | bytes 2359300
  448.2 8.5 %copy-start.46 = (bf16[1024,2,192]{0,2,1:T(8,128)(2,1)S(1)}, bf16[1024,2,192]{0,2,1:T(8,128)(2,1)}, u32[]{:S(2)}) copy-start(bf16[1024,2,192]{0,2,1:T(8,128)(2,1)} %copy-done.45) | copy-start | bytes 2359300
  489.5 328.4 %all-reduce.10.cloned.1.call-start = ((), (), s32[]{:S(2)}) async-start(), calls=%async_computation.13 | async-start | bytes 14155776 | tf_op jit(solution)/shard_map/psum | solution.py:152
  489.8 7.1 copy-start.11
  489.9 8.7 %copy-start.40 = (bf16[1024,2,768]{2,0,1:T(8,128)(2,1)S(1)}, bf16[1024,2,768]{2,0,1:T(8,128)(2,1)}, u32[]{:S(2)}) copy-start(bf16[1024,2,768]{2,0,1:T(8,128)(2,1)} %all-gather.5.cloned.1.call-done) | copy-start | bytes 9437188
  496.9 1.7 copy-start.20
  496.9 1.7 copy-start.22
  496.9 1.7 copy-start.44
  501.8 1.8 copy-start.35
  501.8 1.8 copy-start.33
  501.9 1.7 copy-start.8
  818.0 3.0 copy-start.25
  818.0 3.8 copy-start.13
  821.8 2.5 copy-start.12
  824.3 2.4 copy-start.14
  824.3 3.8 copy-start.1
Sparse Core Ops, SparseCore 0:
  12.2 66.1 all-gather.4
  89.9 58.9 reduce-scatter.4
  153.2 63.4 all-gather.6
  218.8 62.1 all-gather.8
  295.1 58.9 reduce-scatter.8
  358.5 63.4 all-gather.10
  439.4 58.9 reduce-scatter.10
  500.6 60.2 reduce-scatter.6
  566.9 134.1 all-reduce.7
  705.6 112.3 all-reduce.9
where the time goes:
time: 845 us; the launch traced here: 835 us
  waiting for transfers between devices  605 us (72%)
  local copies, waits for them, and re-layouts  78.7 us (9%)
  matrix products  75.1 us (9%)
  blocking collectives  40.5 us (5%)
  other arithmetic  19.7 us (2%)
  between operations  15.1 us (2%)
    psum x1, waiting for transfers between devices, per_device(): lax.psum((grad_qkv, grad_out, up_weight_gradient, down_weight_gradient),...  117 us
    psum x1, waiting for transfers between devices, per_device(): lax.psum((grad_gain_one, grad_gain_two, grad_pair), ('batch', 'tensor'))  93 us
    all_gather x1, waiting for transfers between devices, per_device(): lax.all_gather(grad_middle.astype(jnp.bfloat16), 'tensor', axis=0, tiled=...  63.4 us
    all_gather x1, waiting for transfers between devices, per_device(): lax.all_gather(second_normalized.astype(jnp.bfloat16), 'tensor', axis=0,...  61 us
    reduce_scatter x1, waiting for transfers between devices, per_device(): lax.psum_scatter(jnp.einsum('mwv,gv->mwg', selected_rows, up_projection_w...  59 us
    reduce_scatter x1, waiting for transfers between devices, per_device(): lax.psum_scatter(jnp.einsum('trc,cd->trd', selected_rows, out_weight, pre...  58.4 us
    all_gather x1, waiting for transfers between devices, per_device(): cotangent_block = lax.all_gather(cotangent, 'tensor', axis=0, tiled=True)  57 us
    reduce_scatter x1, waiting for transfers between devices, per_device(): lax.psum_scatter(jnp.einsum('qoa,aj->qoj', selected_rows, down_projection...  56.4 us
  transfers between devices with their start and end apart: 10, of which 9 were waited for; matrix products, arithmetic and copies ran while one was open for 13% of the time, Pallas kernels for 0%

commit v1 on v0

v1 whole, which is shorter than its diff:
```python
import functools

import jax
import jax.numpy as jnp
from jax import lax
from jax.experimental import pallas as pl
from jax.experimental.pallas import tpu as pltpu
from jax.sharding import PartitionSpec as P

MESH = pl.DeviceIdType.MESH
BF = jnp.bfloat16
F32 = jnp.float32
GELU_A = 0.044715
GELU_C = 0.7978845608028654
VMEM_BYTES = 63 << 20


def dot(a, b, ca, cb):
    return lax.dot_general(a, b, (((ca,), (cb,)), ((), ())), preferred_element_type=F32)


def nn(a, b):
    return dot(a, b, 1, 0)


def nt(a, b):
    return dot(a, b, 1, 1)


def tn(a, b):
    return dot(a, b, 0, 0)


def norm_parts(v):
    shifted = v - jnp.mean(v, axis=-1, keepdims=True)
    rstd = lax.rsqrt(jnp.mean(shifted * shifted, axis=-1, keepdims=True) + 1e-05)
    return shifted * rstd, rstd


def kernel(
    tiles,
    bits,
    length,
    n_sems,
    len_ref,
    x_ref,
    cot_ref,
    gain1_ref,
    gain2_ref,
    w0_in,
    w1_in,
    w2_in,
    bias_in,
    mixed_ref,
    gin_ref,
    gains_ref,
    f_out,
    fp_out,
    W0,
    W1,
    W2,
    G1,
    G2,
    R1,
    R2,
    n1,
    pairs,
    gates,
    ratio,
    dinv,
    mid,
    act,
    n2,
    mix,
    gs,
    gn2,
    hr,
    band,
    GP,
    RP,
    FP,
    CS,
    CSR,
    far,
    GA,
    GR,
    UPP,
    ssem,
    rsem,
    lsem,
    ready,
    upper_ready,
):
    T = tiles
    rows, tile, depth = cot_ref.shape
    piece = W1.shape[4]
    half = piece // 2
    b = lax.axis_index("batch")
    z = lax.axis_index("tensor")
    c = lax.rem(b, 2)
    x = lax.rem(b // 2, 2)
    y = lax.rem(b // 4, 2)
    gh = mixed_ref

    def flip(k):
        q = lax.rem(b // (1 << k), 2)
        return (b + (1 << k) - 2 * (1 << k) * q, z)

    core, xp, yp = flip(0), flip(1), flip(2)
    counter = [0]

    def take(n):
        counter[0] += n
        assert counter[0] <= n_sems
        return counter[0] - n

    def rc(src, dst, sem, dev):
        return pltpu.make_async_remote_copy(
            src_ref=src,
            dst_ref=dst,
            send_sem=ssem.at[sem],
            recv_sem=rsem.at[sem],
            device_id=dev,
            device_id_type=MESH,
        )

    def slab(i):
        return lax.rem(z + i, T)

    lo, hi = pl.ds(0, half), pl.ds(half, half)
    partners = [flip(k) for k in range(bits)] + [(b, slab(i)) for i in range(1, T)]

    def w_at(g, j):
        return W0.at[:, :, j] if g == 0 else (W1, W2)[g - 1].at[j]

    w_in = (w0_in, w1_in, w2_in)
    local = [pltpu.make_async_copy(w_in[g], w_at(g, z), lsem.at[g]) for g in range(3)]
    window = bias_in.shape[1]
    bias = gn2.at[0, :, pl.ds(0, window)]
    local.append(pltpu.make_async_copy(bias_in.at[pl.ds(z * tile, tile)], bias, lsem.at[3]))
    local.append(pltpu.make_async_copy(x_ref, n1.at[:, 1], lsem.at[4]))
    for cp in local:
        cp.start()

    barrier = pltpu.get_barrier_semaphore()
    for dev in partners:
        pl.semaphore_signal(barrier, inc=1, device_id=dev, device_id_type=MESH)
    pl.semaphore_wait(barrier, len(partners))

    z_base, a1_base, a2_base, a3_base = take(3 * T), take(6 * T), take(6 * T), take(3 * T)

    def ag_z(g, i):
        dst = W0.at[y, x, z, c] if g == 0 else (W1, W2)[g - 1].at[z, y, x, c]
        return rc(w_in[g].at[y, x, c], dst, z_base + g * T + i, (b, slab(i)))

    def ag_1(g, i, h):
        j = slab(T - i)
        rng = (lo, hi)[h]
        ref = W0.at[y, x, j, c, rng] if g == 0 else (W1, W2)[g - 1].at[j, y, x, c, rng]
        return rc(ref, ref, a1_base + (g * 2 + h) * T + i, (xp, yp)[h])

    def ag_2(g, i, h):
        j = slab(T - i)
        W = (W0, W1, W2)[g]
        if h == 0:
            ref = W.at[y, :, j, c, lo] if g == 0 else W.at[j, y, :, c, lo]
        else:
            ref = W.at[:, x, j, c, hi] if g == 0 else W.at[j, :, x, c, hi]
        return rc(ref, ref, a2_base + (g * 2 + h) * T + i, (yp, xp)[h])

    def ag_3(g, i):
        j = slab(T - i)
        ref = W0.at[:, :, j, c] if g == 0 else (W1, W2)[g - 1].at[j, :, :, c]
        return rc(ref, ref, a3_base + g * T + i, core)

    others = range(1, T)

    def ag_start_z(g):
        for i in others:
            ag_z(g, i).start()

    def ag_step_1(g):
        for i in others:
            ag_z(g, i).wait()
            for h in range(2):
                ag_1(g, i, h).start()

    def ag_step_2(g):
        for i in others:
            for h in range(2):
                ag_1(g, i, h).wait()
                ag_2(g, i, h).start()

    def ag_step_3(g):
        for i in others:
            for h in range(2):
                ag_2(g, i, h).wait()
            ag_3(g, i).start()

    def ag_end(g):
        for i in others:
            ag_3(g, i).wait()

    halo_base = take(4)

    def halo_right():
        return rc(x_ref, n1.at[:, 0], halo_base, (b, lax.min(z + 1, T - 1)))

    def halo_left():
        return rc(x_ref, n1.at[:, 2], halo_base + 1, (b, lax.max(z - 1, 0)))

    ag_start_z(0)
    pl.when(z < T - 1)(lambda: halo_right().start())
    pl.when(z > 0)(lambda: halo_left().start())

    @pl.when(z == 0)
    def _():
        n1[:, 0] = jnp.zeros((rows, tile, depth), BF)
        hr[0] = jnp.zeros((rows, tile, depth), BF)

    @pl.when(z == T - 1)
    def _():
        n1[:, 2] = jnp.zeros((rows, tile, depth), BF)
        hr[1] = jnp.zeros((rows, tile, depth), BF)

    gain1 = gain1_ref[...]
    gain2 = gain2_ref[...]

    def loop(n, body):
        def step(i, carry):
            body(i)
            return carry

        lax.fori_loop(0, n, step, 0)

    def norm_tile(r, t):
        xhat, _ = norm_parts(n1[r, t].astype(F32))
        n1[r, t] = (xhat * gain1).astype(BF)

    local[3].wait()
    wide = jnp.concatenate([jnp.exp(bias[...]), jnp.ones((tile, 3 * tile - window), F32)], axis=1)
    band[...] = pltpu.roll(wide, 0, 1, stride=1, stride_axis=0).astype(BF)
    local[4].wait()
    loop(rows, lambda r: norm_tile(r, 1))

    def mat(ref):
        return ref[...].reshape(depth, depth)

    Wq, Wk, Wv, Wo = W0.at[0, 0], W0.at[0, 1], W0.at[1, 0], W0.at[1, 1]

    ag_step_1(0)
    ag_start_z(1)
    ag_step_2(0)
    ag_step_3(0)
    ag_step_1(1)
    ag_start_z(2)
    ag_end(0)
    local[0].wait()

    def key_values(r, t):
        n = n1[r, t]
        pos = (z - 1 + t) * tile + lax.broadcasted_iota(jnp.int32, (tile, 1), 0)
        keep = (pos >= 0) & (pos < length) & (pos < len_ref[r])
        e = jnp.where(keep, jnp.exp(nt(n, mat(Wk))), 0.0)
        v = nt(n, mat(Wv))
        pairs[r, t, :, pl.ds(0, depth)] = (e * v).astype(BF)
        pairs[r, t, :, pl.ds(depth, depth)] = e.astype(BF)

    def own_qkv(r):
        gates[r] = jax.nn.sigmoid(nt(n1[r, 1], mat(Wq)))
        key_values(r, 1)

    loop(rows, own_qkv)
    ag_step_2(1)

    ones = jnp.ones((8, tile), BF)
    row_of = lax.broadcasted_iota(jnp.int32, (8, 1), 0)
    cs_base = take(2 * T)

    def cs_send(k, i):
        return rc(CS.at[k], CSR.at[k, i - 1], cs_base + k * T + i, (b, slab(i)))

    def cs_start(k, first, second):
        CS[k] = jnp.where(row_of == 0, first, second)
        for i in others:
            cs_send(k, i).start()

    def cs_finish(k):
        total = jnp.zeros(far.shape[1:], F32)
        for i in others:
            cs_send(k, i).wait()
            distance = lax.abs(lax.rem(z - i + T, T) - z)
            total = total + jnp.where(distance >= 2, CSR[k, i - 1], 0.0)
        far[k] = total

    cs_start(0, nn(ones, pairs[0, 1]), nn(ones, pairs[1, 1]))

    pl.when(z < T - 1)(lambda: halo_right().wait_send())
    pl.when(z > 0)(lambda: halo_left().wait_send())
    pl.when(z > 0)(lambda: halo_right().wait_recv())
    pl.when(z < T - 1)(lambda: halo_left().wait_recv())

    def halo_kv(i):
        r = lax.rem(i, rows)
        t = 2 * (i // rows)
        norm_tile(r, t)
        key_values(r, t)

    loop(2 * rows, halo_kv)
    ag_step_3(1)
    ag_step_1(2)
    cs_finish(0)

    x_again = pltpu.make_async_copy(x_ref, act, lsem.at[4])
    x_again.start()

    def mixer(r):
        denom = nn(band[...], pairs[r, :, :, pl.ds(depth, depth)].reshape(3 * tile, depth))
        denom = denom + far[0, pl.ds(r, 1), pl.ds(depth, depth)]
        di = 1.0 / denom
        dinv[r] = di
        numer = nn(band[...], pairs[r, :, :, pl.ds(0, depth)].reshape(3 * tile, depth))
        rt = (numer + far[0, pl.ds(r, 1), pl.ds(0, depth)]) * di
        ratio[r] = rt
        mix[r] = (gates[r] * rt).astype(BF)

    loop(rows, mixer)
    ag_step_2(2)
    x_again.wait()

    def middle(r):
        m = act[r].astype(F32) + nn(mix[r], mat(Wo))
        mid[r] = m
        gin_ref[r] = m
        xhat, _ = norm_parts(m)
        n2[r] = (xhat * gain2).astype(BF)
        gn2[r] = jnp.zeros((tile, depth), F32)

    loop(rows, middle)
    ag_end(1)
    ag_step_3(2)
    local[1].wait()
    local[2].wait()
    ag_end(2)

    G = (W1, G1, G2)
    R = (W2, R1, R2)
    s1_base, s2_base, s3_base, sz_base, f_base = take(3 * 4), take(6 * T), take(6 * T), take(3 * T), take(15)

    def s1(g, i):
        j = slab(i + 1)
        return rc(G[g].at[j, :, :, 1 - c], R[g].at[j, :, :, 0], s1_base + g * 4 + i, core)

    def s1_kind(ty, tx):
        return rc(G[0].at[:, ty, tx, 1 - c], R[0].at[:, ty, tx, 0], s1_base + 2 * ty + tx, core)

    def s2(g, i, h):
        j = slab(i + 1)
        if h == 0:
            src, dst, dev = G[g].at[j, :, 1 - x, c, lo], R[g].at[j, 0, :, 1, lo], xp
        else:
            src, dst, dev = G[g].at[j, 1 - y, :, c, hi], R[g].at[j, 0, :, 1, hi], yp
        return rc(src, dst, s2_base + (g * 2 + h) * T + i, dev)

    def s3(g, i, h):
        j = slab(i + 1)
        if h == 0:
            src, dst, dev = G[g].at[j, 1 - y, x, c, lo], R[g].at[j, 1, 0, 1, lo], yp
        else:
            src, dst, dev = G[g].at[j, y, 1 - x, c, hi], R[g].at[j, 1, 0, 1, hi], xp
        return rc(src, dst, s3_base + (g * 2 + h) * T + i, dev)

    def sz(g, i):
        return rc(G[g].at[slab(i + 1), y, x, c], R[g].at[i, 1, 1, 1], sz_base + g * T + i, (b, slab(i + 1)))

    def add_s1(g, i):
        j = slab(i + 1)
        G[g][j, :, :, c] = G[g][j, :, :, c] + R[g][j, :, :, 0]
        for h in range(2):
            s2(g, i, h).start()

    def s1_finish(g, i):
        s1(g, i).wait()
        add_s1(g, i)

    def s2_finish(g, i):
        j = slab(i + 1)
        s2(g, i, 0).wait()
        G[g][j, :, x, c, lo] = G[g][j, :, x, c, lo] + R[g][j, 0, :, 1, lo]
        s3(g, i, 0).start()
        s2(g, i, 1).wait()
        G[g][j, y, :, c, hi] = G[g][j, y, :, c, hi] + R[g][j, 0, :, 1, hi]
        s3(g, i, 1).start()

    def s3_finish(g, i):
        j = slab(i + 1)
        s3(g, i, 0).wait()
        s3(g, i, 1).wait()
        G[g][j, y, x, c] = G[g][j, y, x, c] + R[g][j, 1, 0, 1]
        if i < T - 1:
            sz(g, i).start()

    def f_at(g):
        return G[g].at[:, :, :, 1 - c]

    def f1(g, h):
        rng = (lo, hi)[h]
        other = f_at(g).at[c, y, x, rng]
        return rc(other, other, f_base + 5 * g + h, (xp, yp)[h])

    def f2(g, h):
        ref = f_at(g).at[c, y, :, lo] if h == 0 else f_at(g).at[c, :, x, hi]
        return rc(ref, ref, f_base + 5 * g + 2 + h, (yp, xp)[h])

    def f3(g):
        return rc(f_at(g).at[c], G[g].at[c, :, :, c], f_base + 5 * g + 4, core)

    u_base = take(4 * max(bits - 3, 0))

    def z_finish(g):
        total = G[g][z, y, x, c].astype(F32)
        for i in range(T - 1):
            sz(g, i).wait()
            total = total + R[g][i, 1, 1, 1].astype(F32)
        mine = f_at(g).at[c, y, x]
        mine[...] = total.astype(BF)
        for k in range(3, bits):
            u = k - 3
            slot = f_at(g).at[2 + u // 4, u // 2 % 2, u % 2]
            pl.semaphore_signal(upper_ready.at[g, u], inc=1, device_id=flip(k), device_id_type=MESH)
            pl.semaphore_wait(upper_ready.at[g, u], 1)
            cp = rc(mine, slot, u_base + g * (bits - 3) + u, flip(k))
            cp.start()
            cp.wait()
            mine[...] = mine[...] + slot[...]
        for h in range(2):
            f1(g, h).start()

    def f1_finish(g):
        for h in range(2):
            f1(g, h).wait()
            f2(g, h).start()

    def f2_finish(g):
        for h in range(2):
            f2(g, h).wait()
        f3(g).start()

    def out_copy(g, k):
        src = G[g].at[k, :, :, 1 - c]
        return pltpu.make_async_copy(src, f_out.at[g, :, :, k], lsem.at[5 + 2 * g + k])

    def f3_finish(g):
        f3(g).wait()
        for k in range(2):
            out_copy(g, k).start()

    def feed(i):
        j = slab(i + 1)
        up, down = W1.at[j], W2.at[j]

        def part(r):
            for k in range(3):
                cols = pl.ds(k * (depth // 3), depth // 3)
                h = nn(n2[r], up[:, :, :, :, cols].reshape(depth, depth // 3))
                ga = nt(cot_ref[r], down[...].reshape(depth, depth)[k * (depth // 3) : (k + 1) * (depth // 3)])
                sq = h * h
                t = jnp.tanh(GELU_C * h * (1.0 + GELU_A * sq))
                hh = 0.5 * h
                act[r, :, cols] = (hh + hh * t).astype(BF)
                slope = 0.5 + 0.5 * t + hh * (1.0 - t * t) * (GELU_C + (3.0 * GELU_C * GELU_A) * sq)
                gh[r, :, cols] = (ga * slope).astype(BF)
            gin_ref[r] += nn(act[r], mat(down))
            gn2[r] += nt(gh[r], mat(up))

        loop(rows, part)
        for m in range(2):
            cols = pl.ds(m * (depth // 2), depth // 2)
            d = tn(act[:, :, cols].reshape(rows * tile, depth // 2), cot_ref[...].reshape(rows * tile, depth))
            G2[j, m] = d.astype(BF).reshape(2, 2, piece, depth)
            d = tn(n2[:, :, cols].reshape(rows * tile, depth // 2), gh[...].reshape(rows * tile, depth))
            G1[j, m] = d.astype(BF).reshape(2, 2, piece, depth)
        s1(1, i).start()
        s1(2, i).start()

        @pl.when(i > 0)
        def _():
            s1_finish(1, i - 1)
            s1_finish(2, i - 1)

    loop(T, feed)
    for dev in partners:
        pl.semaphore_signal(ready, inc=1, device_id=dev, device_id_type=MESH)
    s1_finish(1, T - 1)
    s1_finish(2, T - 1)

    def norm_two_back(r, carry):
        mixed_ref[r] = gin_ref[r].astype(BF)
        xhat, rstd = norm_parts(mid[r])
        grad = gn2[r]
        carry = carry + jnp.sum(grad * xhat, axis=0, keepdims=True)
        g = grad * gain2
        back = g - jnp.mean(g, axis=-1, keepdims=True) - xhat * jnp.mean(g * xhat, axis=-1, keepdims=True)
        gm = cot_ref[r].astype(F32) + rstd * back
        mid[r] = gm
        n2[r] = gm.astype(BF)
        return carry

    gain2_grad = lax.fori_loop(0, rows, norm_two_back, jnp.zeros((1, depth), F32))

    for i in range(T):
        s2_finish(1, i)
        s2_finish(2, i)
    pl.semaphore_wait(ready, len(partners))

    local[3].start()

    def kind(ty, tx, lhs, start, rhs):
        for m in range(2):
            part = lhs[..., pl.ds(start + m * (depth // 2), depth // 2)]
            d = tn(part.reshape(rhs.shape[0], depth // 2), rhs).astype(BF)
            d = d.reshape(2, 2, piece, depth)
            for s in range(2):
                G[0][2 * m + s, ty, tx] = d[s]
        s1_kind(ty, tx).start()

    flat = (rows * tile, depth)
    kind(1, 1, mix, 0, n2[...].reshape(flat))

    def mixer_back(r):
        gmix = nt(n2[r], mat(Wo))
        gate = gates[r]
        rt = ratio[r]
        first = gmix * gate
        act[r] = (first * rt * (1.0 - gate)).astype(BF)
        first = first * dinv[r]
        gs[r, :, pl.ds(0, depth)] = first.astype(BF)
        gs[r, :, pl.ds(depth, depth)] = (-first * rt).astype(BF)

    loop(rows, mixer_back)
    cs_start(1, nn(ones, gs[0]), nn(ones, gs[1]))
    kind(0, 0, act, 0, n1[:, 1].reshape(flat))

    for i in range(T):
        s3_finish(1, i)
        s3_finish(2, i)

    local[3].wait()
    gband = nt(gs[0], pairs[0].reshape(3 * tile, 2 * depth)) + nt(gs[1], pairs[1].reshape(3 * tile, 2 * depth))
    shift = lax.broadcasted_iota(jnp.int32, (tile, 1), 0)
    k = 1
    while k < tile:
        gband = jnp.where(lax.rem(shift // k, 2) == 1, pltpu.roll(gband, 3 * tile - k, 1), gband)
        k *= 2
    gp = (gband[:, :window] * jnp.exp(bias[...])).astype(BF)
    GP[...] = gp.reshape(GP.shape)
    p_base = take(6 + T)
    up_base = u_base + 3 * max(bits - 3, 0)

    def p1():
        return rc(GP.at[:, :, 1 - c], RP.at[:, :, 0], p_base, core)

    def p2():
        return rc(GP.at[:, 1 - x, c], RP.at[0, :, 1], p_base + 1, xp)

    def p3():
        return rc(GP.at[1 - y, x, c], RP.at[1, 0, 1], p_base + 2, yp)

    def pz(i):
        mine = FP.at[z, y, x, c]
        return rc(mine, mine, p_base + 6 + i, (b, slab(i)))

    def pa1():
        ref = FP.at[:, y, x, c]
        return rc(ref, ref, p_base + 3, xp)

    def pa2():
        ref = FP.at[:, y, :, c]
        return rc(ref, ref, p_base + 4, yp)

    def pa3():
        ref = FP.at[:, :, :, c]
        return rc(ref, ref, p_base + 5, core)

    p1().start()
    z_finish(1)
    z_finish(2)
    cs_finish(1)

    def pairs_back(r):
        for t in range(3):
            near = band[:, pl.ds(t * tile, tile)]
            gn = tn(near, gs[r, :, pl.ds(0, depth)])
            gd = tn(near, gs[r, :, pl.ds(depth, depth)])
            if t == 1:
                gn = gn + far[1, pl.ds(r, 1), pl.ds(0, depth)]
                gd = gd + far[1, pl.ds(r, 1), pl.ds(depth, depth)]
            wv = pairs[r, t, :, pl.ds(0, depth)].astype(F32)
            we = pairs[r, t, :, pl.ds(depth, depth)].astype(F32)
            pairs[r, t, :, pl.ds(0, depth)] = (gn * wv + gd * we).astype(BF)
            pairs[r, t, :, pl.ds(depth, depth)] = (gn * we).astype(BF)

    loop(rows, pairs_back)
    p1().wait()
    GP[:, :, c] = GP[:, :, c] + RP[:, :, 0]
    p2().start()

    n1_all = n1[...].reshape(3 * rows * tile, depth)
    kind(0, 1, pairs, 0, n1_all)
    f1_finish(1)
    f1_finish(2)
    kind(1, 0, pairs, depth, n1_all)
    p2().wait()
    GP[:, x, c] = GP[:, x, c] + RP[0, :, 1]
    p3().start()
    for ty in range(2):
        for tx in range(2):
            s1_kind(ty, tx).wait()
    for i in range(T):
        add_s1(0, i)

    def halo_part(d):
        def body(r):
            g = nn(pairs[r, 2 * d, :, pl.ds(0, depth)], mat(Wk))
            g = g + nn(pairs[r, 2 * d, :, pl.ds(depth, depth)], mat(Wv))
            gs[r, :, pl.ds(d * depth, depth)] = g.astype(BF)

        loop(rows, body)

    def back_left():
        return rc(gs.at[:, :, pl.ds(0, depth)], hr.at[1], halo_base + 2, (b, lax.max(z - 1, 0)))

    def back_right():
        return rc(gs.at[:, :, pl.ds(depth, depth)], hr.at[0], halo_base + 3, (b, lax.min(z + 1, T - 1)))

    halo_part(0)
    pl.when(z > 0)(lambda: back_left().start())
    halo_part(1)
    pl.when(z < T - 1)(lambda: back_right().start())
    for i in range(T):
        s2_finish(0, i)

    def own_grad(r):
        g = nn(act[r], mat(Wq)) + nn(pairs[r, 1, :, pl.ds(0, depth)], mat(Wk))
        gin_ref[r] = g + nn(pairs[r, 1, :, pl.ds(depth, depth)], mat(Wv))

    loop(rows, own_grad)
    x_again.start()
    f2_finish(1)
    f2_finish(2)
    p3().wait()
    GP[y, x, c] = GP[y, x, c] + RP[1, 0, 1]
    for k in range(3, bits):
        cp = rc(GP.at[y, x, c], UPP.at[k - 3], up_base + k - 3, flip(k))
        cp.start()
        cp.wait()
        GP[y, x, c] = GP[y, x, c] + UPP[k - 3]
    FP[z, y, x, c] = GP[y, x, c]
    for i in others:
        pz(i).start()
    for i in range(T):
        s3_finish(0, i)

    pl.when(z > 0)(lambda: back_left().wait_send())
    pl.when(z < T - 1)(lambda: back_right().wait_send())
    pl.when(z < T - 1)(lambda: back_left().wait_recv())
    pl.when(z > 0)(lambda: back_right().wait_recv())
    x_again.wait()

    def norm_one_back(r, carry):
        xhat, rstd = norm_parts(act[r].astype(F32))
        grad = gin_ref[r] + hr[0, r].astype(F32) + hr[1, r].astype(F32)
        carry = carry + jnp.sum(grad * xhat, axis=0, keepdims=True)
        g = grad * gain1
        back = g - jnp.mean(g, axis=-1, keepdims=True) - xhat * jnp.mean(g * xhat, axis=-1, keepdims=True)
        gin_ref[r] = mid[r] + rstd * back
        return carry

    gain1_grad = lax.fori_loop(0, rows, norm_one_back, jnp.zeros((1, depth), F32))

    g_base = take(bits + T)
    GA[0] = jnp.where(row_of == 0, gain1_grad, gain2_grad)

    def ga(k):
        return rc(GA.at[k], GR.at[k], g_base + k, flip(k))

    def gz(i):
        return rc(GA.at[bits], GR.at[bits + z], g_base + bits + i, (b, slab(i)))

    def gains_step(k):
        ga(k).wait()
        GA[k + 1] = GA[k] + GR[k]
        if k + 1 < bits:
            ga(k + 1).start()
        else:
            GR[bits + z] = GA[bits]
            for i in others:
                gz(i).start()

    ga(0).start()
    f3_finish(1)
    f3_finish(2)
    gains_step(0)
    for i in others:
        pz(i).wait()
    pa1().start()
    gains_step(1)
    z_finish(0)
    gains_step(2)
    for k in range(3, bits):
        gains_step(k)
    pa1().wait()
    pa2().start()
    f1_finish(0)
    for i in others:
        gz(i).wait()
    total = GR[bits]
    for i in range(1, T):
        total = total + GR[bits + i]
    gains_ref[...] = total
    pa2().wait()
    pa3().start()
    f2_finish(0)
    pa3().wait()
    fp_copy = pltpu.make_async_copy(FP, fp_out, lsem.at[3])
    fp_copy.start()
    f3_finish(0)
    for g in range(3):
        for k in range(2):
            out_copy(g, k).wait()
    fp_copy.wait()


def per_device(
    tiles,
    batch,
    inputs,
    lengths,
    gain_one,
    qkv_weight,
    out_weight,
    gain_two,
    up_projection_weight,
    down_projection_weight,
    pair_bias,
    cotangent,
):
    tile, rows, depth = inputs.shape
    bits = batch.bit_length() - 1
    channels = qkv_weight.shape[2]
    piece = depth // 8
    window = pair_bias.shape[1]
    strip = tile // 8
    x = jnp.transpose(inputs, (1, 0, 2))
    cot = jnp.transpose(cotangent, (1, 0, 2))
    cut = (2, 2, 2, piece, depth)
    w0 = jnp.concatenate([jnp.transpose(qkv_weight, (0, 2, 1)), out_weight[None]]).reshape(cut)
    w1 = up_projection_weight.reshape(cut)
    w2 = down_projection_weight.reshape(cut)
    n_sems = 256 if bits == 3 else 288
    tokens = (rows, tile, depth)
    T = tiles
    vmem = pl.BlockSpec(memory_space=pltpu.VMEM)
    hbm = pl.BlockSpec(memory_space=pl.ANY)
    blocks = (T, 2, 2, 2, piece, depth)
    upper = max(bits - 3, 1)
    scratch = [
        pltpu.VMEM((2, 2, T, 2, piece, depth), BF),
        pltpu.VMEM(blocks, BF),
        pltpu.VMEM(blocks, BF),
        pltpu.VMEM(blocks, BF),
        pltpu.VMEM(blocks, BF),
        pltpu.VMEM(blocks, BF),
        pltpu.VMEM(blocks, BF),
        pltpu.VMEM((rows, 3, tile, depth), BF),
        pltpu.VMEM((rows, 3, tile, 2 * depth), BF),
        pltpu.VMEM(tokens, F32),
        pltpu.VMEM(tokens, F32),
        pltpu.VMEM(tokens, F32),
        pltpu.VMEM(tokens, F32),
        pltpu.VMEM(tokens, BF),
        pltpu.VMEM(tokens, BF),
        pltpu.VMEM(tokens, BF),
        pltpu.VMEM((rows, tile, 2 * depth), BF),
        pltpu.VMEM(tokens, F32),
        pltpu.VMEM((2,) + tokens, BF),
        pltpu.VMEM((tile, 3 * tile), BF),
        pltpu.VMEM((2, 2, 2, strip, window), BF),
        pltpu.VMEM((2, 2, 2, strip, window), BF),
        pltpu.VMEM((T, 2, 2, 2, strip, window), BF),
        pltpu.VMEM((2, 8, 2 * depth), F32),
        pltpu.VMEM((2, T - 1, 8, 2 * depth), F32),
        pltpu.VMEM((2, 8, 2 * depth), F32),
        pltpu.VMEM((bits + 1, 8, depth), F32),
        pltpu.VMEM((bits + T, 8, depth), F32),
        pltpu.VMEM((upper, strip, window), BF),
        pltpu.SemaphoreType.DMA((n_sems,)),
        pltpu.SemaphoreType.DMA((n_sems,)),
        pltpu.SemaphoreType.DMA((11,)),
        pltpu.SemaphoreType.REGULAR,
        pltpu.SemaphoreType.REGULAR((3, upper)),
    ]
    mixed, grad_inputs, gains, sums, pair = pl.pallas_call(
        functools.partial(kernel, T, bits, T * tile, n_sems),
        out_shape=(
            jax.ShapeDtypeStruct(tokens, BF),
            jax.ShapeDtypeStruct(tokens, F32),
            jax.ShapeDtypeStruct((8, depth), F32),
            jax.ShapeDtypeStruct((3,) + cut, BF),
            jax.ShapeDtypeStruct((T, 2, 2, 2, strip, window), BF),
        ),
        in_specs=[pl.BlockSpec(memory_space=pltpu.SMEM), hbm, vmem, vmem, vmem, hbm, hbm, hbm, hbm],
        out_specs=(vmem, vmem, vmem, hbm, hbm),
        scratch_shapes=scratch,
        compiler_params=pltpu.CompilerParams(
            collective_id=0, has_side_effects=True, vmem_limit_bytes=VMEM_BYTES
        ),
    )(
        lengths,
        x,
        cot,
        gain_one.astype(F32)[None],
        gain_two.astype(F32)[None],
        w0,
        w1,
        w2,
        pair_bias,
    )
    sums = sums.reshape(3, depth, depth).astype(F32)
    first = sums[0].reshape(4, channels, depth)
    return (
        jnp.transpose(mixed, (1, 0, 2)),
        jnp.transpose(grad_inputs, (1, 0, 2)),
        gains[0],
        jnp.transpose(first[:3], (0, 2, 1)),
        first[3],
        gains[1],
        sums[1],
        sums[2],
        pair.reshape(T * tile, window).astype(F32),
    )


def solution(mesh):
    return jax.shard_map(
        functools.partial(per_device, mesh.shape["tensor"], mesh.shape["batch"]),
        mesh=mesh,
        in_specs=(
            P("tensor", "batch", None),
            P("batch"),
            P(),
            P(None, None, "tensor"),
            P("tensor", None),
            P(),
            P(None, "tensor"),
            P("tensor", None),
            P(),
            P("tensor", "batch", None),
        ),
        out_specs=(
            P("tensor", "batch", None),
            P("tensor", "batch", None),
            P(),
            P(None, None, "tensor"),
            P("tensor", None),
            P(),
            P(None, "tensor"),
            P("tensor", None),
            P(),
        ),
        check_vma=False,
    )
```

time: 845 us -> 239 us (0.28)
  waiting for transfers between devices: 605 us -> 0 us
  Pallas kernels: 0 us -> 213 us
  matrix products: 75.1 us -> 0 us
  local copies, waits for them, and re-layouts: 78.7 us -> 17 us
  blocking collectives: 40.5 us -> 0 us
  other arithmetic: 19.7 us -> 3.64 us
  between operations: 15.1 us -> 0.71 us
    all_gather x4 -> x0, waiting for transfers between devices: 221 us -> none  [the longest x1 63.4 us: per_device(): lax.all_gather(grad_middle.astype(jnp.bfloat16), 'tensor', axis=0, tiled=...]
    pallas_call x0 -> x1, Pallas kernels: none -> 213 us  [per_device(): pl.pallas_call(functools.partial(kernel, T, bits, T * tile, n_sems), out_...]
    psum x2 -> x0, waiting for transfers between devices: 210 us -> none  [the longest x1 117 us: per_device(): lax.psum((grad_qkv, grad_out, up_weight_gradient, down_weight_gradient),...]
    reduce_scatter x4 -> x0, waiting for transfers between devices: 174 us -> none  [the longest x1 59 us: per_device(): lax.psum_scatter(jnp.einsum('mwv,gv->mwg', selected_rows, up_projection_w...]
    dot_general x15 -> x0, matrix products: 75.1 us -> none  [the longest x1 8.56 us: per_device(): jnp.einsum('qoa,aj->qoj', selected_rows, down_projection_weight, preferre...]
    psum x1 -> x0, blocking collectives: 40.5 us -> none  [per_device(): lax.psum((grad_gain_one, grad_gain_two, grad_pair), ('batch', 'tensor'))]
    reshape x4 -> x0, local copies, waits for them, and re-layouts: 34.8 us -> none  [the longest x1 10.4 us: band_pick(): return flat.reshape(length, length + doubled + 1)[:, :doubled]]
    unnamed x106 -> x14, local copies, waits for them, and re-layouts: 23.2 us -> 6.76 us
  transfers between devices with their start and end apart: 10 -> 0, of which waited for: 9 -> 0; matrix products, arithmetic and copies ran while one was open for 13% -> 0% of each run, Pallas kernels for 0% -> 0%
where the time goes in v1:
time: 239 us; the launch traced here: 234 us
  Pallas kernels  213 us (89%)
  local copies, waits for them, and re-layouts  17 us (7%)
  other arithmetic  3.64 us (2%)
    pallas_call x1, Pallas kernels, per_device(): pl.pallas_call(functools.partial(kernel, T, bits, T * tile, n_sems), out_...  213 us
    unnamed x14, local copies, waits for them, and re-layouts  6.76 us

profile of v1, /device:TPU:0, one launch (start us, length us, event | category | flops | bytes accessed | tf_op | source)
XLA Modules:
  0.0 234.1 jit_solution(2487474128319225528)
XLA Ops:
  0.6 0.0 copy-start.4
  0.7 0.0 copy-start.5
  0.7 0.0 copy-start.3
  0.7 0.0 copy-start.2
  0.7 2.8 %copy_bitcast_fusion = (bf16[2,256,768]{2,1,0:T(8,128)(2,1)}, bf16[2,256,768]{2,1,0:T(8,128)(2,1)}) fusion(bf16[256,2,768]{2,1,0:T(2,128)(2,1)} %param.19, bf16[256,2,768]{2,1,0:T(2,128)(2,1)} %param.10), kind=kLoop, calls=%fused_computation.2 | loop fusion | bytes 3145728 | tf_op jit(solution)/shard_map/transpose | solution.py:755
  3.5 0.0 copy-done.4
  3.5 0.6 reshape.42.gain1_ref
  4.1 0.0 copy-done.5
  4.1 0.6 reshape.43.gain2_ref
  4.7 0.0 copy-done.3
  4.7 0.0 copy-done.2
  4.7 1.1 pad_maximum_fusion
  5.8 212.7 %shard_map.169 = (bf16[2,256,768]{2,1,0:T(8,128)(2,1)}, f32[2,256,768]{2,1,0:T(8,128)}, f32[8,768]{1,0:T(8,128)}, bf16[3,2,2,2,96,768]{5,4,3,2,1,0:T(8,128)(2,1)}, bf16[4,2,2,2,32,512]{5,4,3,2,1,0:T(8,128)(2,1)}) custom-call(s32[2]{0:T(128)} %len_ref.1, bf16[2,256,768]{2,1,0:T(8,128)(2,1)} %get-tuple-element.33.x_ref, ...), custom_call_target="tpu_custom_call" | custom-call | tf_op jit(solution)/shard_map/pallas_call | solution.py:803
  218.5 0.0 copy-start
  218.5 3.0 %copy.21 = bf16[256,2,768]{2,1,0:T(2,128)(2,1)} copy(bf16[256,2,768]{2,0,1:T(8,128)(2,1)} %bitcast.32) | data formatting | bytes 1572864
  221.5 3.8 %copy.22 = f32[256,2,768]{2,1,0:T(2,128)} copy(f32[256,2,768]{2,0,1:T(8,128)} %bitcast.28) | data formatting | bytes 3145728
  225.3 1.4 slice_reduce_fusion
  226.7 0.0 copy-done
  226.7 0.8 convert_element_type.14
  227.5 1.3 slice.34
  228.9 0.9 slice_bitcast_fusion
  229.7 0.0 copy-start.1
  229.7 2.7 %fusion = (f32[1,2,2,2,96,768]{5,4,3,2,1,0:T(8,128)}, f32[1,2,2,2,96,768]{5,4,3,2,1,0:T(8,128)}) fusion(bf16[3,2,2,2,96,768]{5,4,3,2,1,0:T(8,128)(2,1)S(1)} %copy-done), kind=kLoop, calls=%fused_computation.7 | loop fusion | bytes 9437184 | tf_op jit(solution)/shard_map/slice | solution.py:839
  232.4 0.0 copy-done.1
  232.4 1.7 bitcast_convert_fusion
Async XLA Ops:
  0.6 2.8 %copy-start.4 = (bf16[768]{0:T(1024)(128)(2,1)S(1)}, bf16[768]{0:T(1024)(128)(2,1)}, u32[]{:S(2)}) copy-start(bf16[768]{0:T(1024)(128)(2,1)} %param.12) | copy-start | bytes 4612
  0.7 3.4 %copy-start.5 = (bf16[768]{0:T(1024)(128)(2,1)S(1)}, bf16[768]{0:T(1024)(128)(2,1)}, u32[]{:S(2)}) copy-start(bf16[768]{0:T(1024)(128)(2,1)} %param.15) | copy-start | bytes 4612
  0.7 4.0 %copy-start.3 = (bf16[192,768]{1,0:T(8,128)(2,1)S(1)}, bf16[192,768]{1,0:T(8,128)(2,1)}, u32[]{:S(2)}) copy-start(bf16[192,768]{1,0:T(8,128)(2,1)} %param.14) | copy-start | bytes 884740
  0.7 4.0 %copy-start.2 = (bf16[3,768,192]{1,2,0:T(8,128)(2,1)S(1)}, bf16[3,768,192]{1,2,0:T(8,128)(2,1)}, u32[]{:S(2)}) copy-start(bf16[3,768,192]{1,2,0:T(8,128)(2,1)} %param.13) | copy-start | bytes 2654212
  218.5 8.2 %copy-start = (bf16[3,2,2,2,96,768]{5,4,3,2,1,0:T(8,128)(2,1)S(1)}, bf16[3,2,2,2,96,768]{5,4,3,2,1,0:T(8,128)(2,1)}, u32[]{:S(2)}) copy-start(bf16[3,2,2,2,96,768]{5,4,3,2,1,0:T(8,128)(2,1)} %get-tuple-element.17) | copy-start | bytes 10616836
  229.7 2.7 %copy-start.1 = (bf16[4,2,2,2,32,512]{5,4,3,2,1,0:T(8,128)(2,1)S(1)}, bf16[4,2,2,2,32,512]{5,4,3,2,1,0:T(8,128)(2,1)}, u32[]{:S(2)}) copy-start(bf16[4,2,2,2,32,512]{5,4,3,2,1,0:T(8,128)(2,1)} %get-tuple-element.18) | copy-start | bytes 3145732

commit v2 on v1

--- a/solution.py
+++ b/solution.py
@@ -114,11 +114,11 @@
         assert counter[0] <= n_sems
         return counter[0] - n
 
-    def rc(src, dst, sem, dev):
+    def rc(src, dst, sem, dev, sent=None):
         return pltpu.make_async_remote_copy(
             src_ref=src,
             dst_ref=dst,
-            send_sem=ssem.at[sem],
+            send_sem=ssem.at[sem if sent is None else sent],
             recv_sem=rsem.at[sem],
             device_id=dev,
             device_id_type=MESH,
@@ -127,6 +127,11 @@
     def slab(i):
         return lax.rem(z + i, T)
 
+    def nth(k):
+        near = [sorted(range(T), key=lambda j: (abs(j - q), j))[k] for q in range(T)]
+        return sum(near[q] * (1 - lax.min(lax.abs(z - q), 1)) for q in range(T))
+
+    slabs = [z] + [nth(k) for k in range(1, T)]
     lo, hi = pl.ds(0, half), pl.ds(half, half)
     partners = [flip(k) for k in range(bits)] + [(b, slab(i)) for i in range(1, T)]
 
@@ -148,70 +153,96 @@
     pl.semaphore_wait(barrier, len(partners))
 
     z_base, a1_base, a2_base, a3_base = take(3 * T), take(6 * T), take(6 * T), take(3 * T)
-
-    def ag_z(g, i):
-        dst = W0.at[y, x, z, c] if g == 0 else (W1, W2)[g - 1].at[z, y, x, c]
-        return rc(w_in[g].at[y, x, c], dst, z_base + g * T + i, (b, slab(i)))
-
-    def ag_1(g, i, h):
-        j = slab(T - i)
-        rng = (lo, hi)[h]
-        ref = W0.at[y, x, j, c, rng] if g == 0 else (W1, W2)[g - 1].at[j, y, x, c, rng]
-        return rc(ref, ref, a1_base + (g * 2 + h) * T + i, (xp, yp)[h])
-
-    def ag_2(g, i, h):
-        j = slab(T - i)
+    own_base = take(6)
+    right, left = (b, lax.min(z + 1, T - 1)), (b, lax.max(z - 1, 0))
+    has_right, has_left = z < T - 1, z > 0
+
+    def piece_at(g, j):
+        return W0.at[y, x, j, c] if g == 0 else (W1, W2)[g - 1].at[j, y, x, c]
+
+    def own_send(g, side):
+        dst = piece_at(g, z)
+        return rc(w_in[g].at[y, x, c], dst, z_base + g * T + z, (right, left)[side], own_base + 2 * g + side)
+
+    def pass_on(g, k, side):
+        ref = piece_at(g, slabs[k])
+        return rc(ref, ref, z_base + g * T + slabs[k], (right, left)[side])
+
+    def ag_1(g, k, h):
+        ref = piece_at(g, slabs[k]).at[(lo, hi)[h]]
+        return rc(ref, ref, a1_base + (g * 2 + h) * T + k, (xp, yp)[h])
+
+    def ag_2(g, k, h):
+        j = slabs[k]
         W = (W0, W1, W2)[g]
         if h == 0:
             ref = W.at[y, :, j, c, lo] if g == 0 else W.at[j, y, :, c, lo]
         else:
             ref = W.at[:, x, j, c, hi] if g == 0 else W.at[j, :, x, c, hi]
-        return rc(ref, ref, a2_base + (g * 2 + h) * T + i, (yp, xp)[h])
-
-    def ag_3(g, i):
-        j = slab(T - i)
+        return rc(ref, ref, a2_base + (g * 2 + h) * T + k, (yp, xp)[h])
+
+    def ag_3(g, k):
+        j = slabs[k]
         ref = W0.at[:, :, j, c] if g == 0 else (W1, W2)[g - 1].at[j, :, :, c]
-        return rc(ref, ref, a3_base + g * T + i, core)
+        return rc(ref, ref, a3_base + g * T + k, core)
 
     others = range(1, T)
 
-    def ag_start_z(g):
-        for i in others:
-            ag_z(g, i).start()
-
-    def ag_step_1(g):
-        for i in others:
-            ag_z(g, i).wait()
+    def z_start(*groups):
+        for side, there in ((0, has_right), (1, has_left)):
+
+            @pl.when(there)
+            def _():
+                for g in groups:
+                    own_send(g, side).start()
+
+    def passing(k):
+        j = slabs[k]
+        return ((0, (j < z) & has_right), (1, (j > z) & has_left))
+
+    def to_1(k, *groups):
+        for g in groups:
+            pass_on(g, k, 0).wait_recv()
+            for side, there in passing(k):
+                pl.when(there)(lambda: pass_on(g, k, side).start())
             for h in range(2):
-                ag_1(g, i, h).start()
-
-    def ag_step_2(g):
-        for i in others:
+                ag_1(g, k, h).start()
+
+    def to_2(k, *groups):
+        for g in groups:
             for h in range(2):
-                ag_1(g, i, h).wait()
-                ag_2(g, i, h).start()
-
-    def ag_step_3(g):
-        for i in others:
+                ag_1(g, k, h).wait()
+                ag_2(g, k, h).start()
+
+    def to_3(k, *groups):
+        for g in groups:
             for h in range(2):
-                ag_2(g, i, h).wait()
-            ag_3(g, i).start()
-
-    def ag_end(g):
-        for i in others:
-            ag_3(g, i).wait()
-
-    halo_base = take(4)
-
-    def halo_right():
-        return rc(x_ref, n1.at[:, 0], halo_base, (b, lax.min(z + 1, T - 1)))
-
-    def halo_left():
-        return rc(x_ref, n1.at[:, 2], halo_base + 1, (b, lax.max(z - 1, 0)))
-
-    ag_start_z(0)
-    pl.when(z < T - 1)(lambda: halo_right().start())
-    pl.when(z > 0)(lambda: halo_left().start())
+                ag_2(g, k, h).wait()
+            ag_3(g, k).start()
+
+    def arrived(k, *groups):
+        for g in groups:
+            ag_3(g, k).wait()
+            for side, there in passing(k):
+                pl.when(there)(lambda: pass_on(g, k, side).wait_send())
+
+    def z_sent(*groups):
+        for side, there in ((0, has_right), (1, has_left)):
+
+            @pl.when(there)
+            def _():
+                for g in groups:
+                    own_send(g, side).wait_send()
+
+    halo_base = take(2 * rows + 2)
+
+    def halo_right(r):
+        return rc(x_ref.at[r], n1.at[r, 0], halo_base + 2 + 2 * r, right)
+
+    def halo_left(r):
+        return rc(x_ref.at[r], n1.at[r, 2], halo_base + 3 + 2 * r, left)
+
+    z_start(0)
 
     @pl.when(z == 0)
     def _():
@@ -248,13 +279,25 @@
 
     Wq, Wk, Wv, Wo = W0.at[0, 0], W0.at[0, 1], W0.at[1, 0], W0.at[1, 1]
 
-    ag_step_1(0)
-    ag_start_z(1)
-    ag_step_2(0)
-    ag_step_3(0)
-    ag_step_1(1)
-    ag_start_z(2)
-    ag_end(0)
+    to_1(1, 0)
+    to_1(2, 0)
+
+    def halo_start():
+        for r in range(rows):
+            pl.when(has_right)(lambda: halo_right(r).start())
+            pl.when(has_left)(lambda: halo_left(r).start())
+
+    to_2(1, 0)
+    to_1(3, 0)
+    halo_start()
+    z_start(1, 2)
+    to_2(2, 0)
+    to_3(1, 0)
+    to_2(3, 0)
+    to_3(2, 0)
+    to_3(3, 0)
+    for k in others:
+        arrived(k, 0)
     local[0].wait()
 
     def key_values(r, t):
@@ -271,7 +314,6 @@
         key_values(r, 1)
 
     loop(rows, own_qkv)
-    ag_step_2(1)
 
     ones = jnp.ones((8, tile), BF)
     row_of = lax.broadcasted_iota(jnp.int32, (8, 1), 0)
@@ -295,20 +337,23 @@
 
     cs_start(0, nn(ones, pairs[0, 1]), nn(ones, pairs[1, 1]))
 
-    pl.when(z < T - 1)(lambda: halo_right().wait_send())
-    pl.when(z > 0)(lambda: halo_left().wait_send())
-    pl.when(z > 0)(lambda: halo_right().wait_recv())
-    pl.when(z < T - 1)(lambda: halo_left().wait_recv())
-
-    def halo_kv(i):
-        r = lax.rem(i, rows)
-        t = 2 * (i // rows)
-        norm_tile(r, t)
-        key_values(r, t)
-
-    loop(2 * rows, halo_kv)
-    ag_step_3(1)
-    ag_step_1(2)
+    def halo_kv(r):
+        @pl.when(z > 0)
+        def _():
+            halo_left(r).wait_send()
+            halo_right(r).wait_recv()
+
+        @pl.when(z < T - 1)
+        def _():
+            halo_right(r).wait_send()
+            halo_left(r).wait_recv()
+
+        for t in (0, 2):
+            norm_tile(r, t)
+            key_values(r, t)
+
+    loop(rows, halo_kv)
+    to_1(1, 1, 2)
     cs_finish(0)
 
     x_again = pltpu.make_async_copy(x_ref, act, lsem.at[4])
@@ -324,8 +369,10 @@
         ratio[r] = rt
         mix[r] = (gates[r] * rt).astype(BF)
 
-    loop(rows, mixer)
-    ag_step_2(2)
+    mixer(0)
+    to_1(2, 1, 2)
+    mixer(1)
+    to_2(1, 1, 2)
     x_again.wait()
 
     def middle(r):
@@ -337,68 +384,91 @@
         gn2[r] = jnp.zeros((tile, depth), F32)
 
     loop(rows, middle)
-    ag_end(1)
-    ag_step_3(2)
     local[1].wait()
     local[2].wait()
-    ag_end(2)
 
     G = (W1, G1, G2)
     R = (W2, R1, R2)
-    s1_base, s2_base, s3_base, sz_base, f_base = take(3 * 4), take(6 * T), take(6 * T), take(3 * T), take(15)
-
-    def s1(g, i):
-        j = slab(i + 1)
-        return rc(G[g].at[j, :, :, 1 - c], R[g].at[j, :, :, 0], s1_base + g * 4 + i, core)
+    s1_base, s2_base, s3_base, sz_base, f_base = take(12), take(24), take(24), take(3 * T), take(15)
+    def s1(g, o):
+        j = slabs[o]
+        return rc(G[g].at[j, :, :, 1 - c], R[g].at[j, :, :, 0], s1_base + g * 4 + o, core)
 
     def s1_kind(ty, tx):
         return rc(G[0].at[:, ty, tx, 1 - c], R[0].at[:, ty, tx, 0], s1_base + 2 * ty + tx, core)
 
-    def s2(g, i, h):
-        j = slab(i + 1)
+    def s2(g, o, h):
+        j = slabs[o]
         if h == 0:
             src, dst, dev = G[g].at[j, :, 1 - x, c, lo], R[g].at[j, 0, :, 1, lo], xp
         else:
             src, dst, dev = G[g].at[j, 1 - y, :, c, hi], R[g].at[j, 0, :, 1, hi], yp
-        return rc(src, dst, s2_base + (g * 2 + h) * T + i, dev)
-
-    def s3(g, i, h):
-        j = slab(i + 1)
+        return rc(src, dst, s2_base + (g * 2 + h) * 4 + o, dev)
+
+    def s2_kind(late, h):
+        if h == 0:
+            k = x if late else 1 - x
+            src, dst, dev = G[0].at[:, k, 1 - x, c, lo], R[0].at[:, 0, k, 1, lo], xp
+        else:
+            k = y if late else 1 - y
+            src, dst, dev = G[0].at[:, 1 - y, k, c, hi], R[0].at[:, 0, k, 1, hi], yp
+        return rc(src, dst, s2_base + h * 4 + late, dev)
+
+    def s3(g, o, h):
+        j = slabs[o]
         if h == 0:
             src, dst, dev = G[g].at[j, 1 - y, x, c, lo], R[g].at[j, 1, 0, 1, lo], yp
         else:
             src, dst, dev = G[g].at[j, y, 1 - x, c, hi], R[g].at[j, 1, 0, 1, hi], xp
-        return rc(src, dst, s3_base + (g * 2 + h) * T + i, dev)
-
-    def sz(g, i):
-        return rc(G[g].at[slab(i + 1), y, x, c], R[g].at[i, 1, 1, 1], sz_base + g * T + i, (b, slab(i + 1)))
-
-    def add_s1(g, i):
-        j = slab(i + 1)
-        G[g][j, :, :, c] = G[g][j, :, :, c] + R[g][j, :, :, 0]
+        return rc(src, dst, s3_base + (g * 2 + h) * 4 + o, dev)
+
+    def sz(g, o):
+        j = lax.rem(z - o + T, T)
+        return rc(G[g].at[j, y, x, c], R[g].at[o - 1, 1, 1, 1], sz_base + g * T + o, (b, j))
+
+    def sz_slab(g, k):
+        j = slabs[k]
+        o = lax.rem(z - j + T, T)
+        return rc(G[g].at[j, y, x, c], R[g].at[o - 1, 1, 1, 1], sz_base + g * T + o, (b, j))
+
+    def s1_finish(o, *groups):
+        j = slabs[o]
+        for g in groups:
+            s1(g, o).wait()
+            G[g][j, :, :, c] = G[g][j, :, :, c] + R[g][j, :, :, 0]
+            for h in range(2):
+                s2(g, o, h).start()
+
+    def s1_kind_finish(ty, tx):
+        s1_kind(ty, tx).wait()
+        G[0][:, ty, tx, c] = G[0][:, ty, tx, c] + R[0][:, ty, tx, 0]
+
+    def s2_finish(o, *groups):
+        j = slabs[o]
+        for g in groups:
+            s2(g, o, 0).wait()
+            G[g][j, :, x, c, lo] = G[g][j, :, x, c, lo] + R[g][j, 0, :, 1, lo]
+            s3(g, o, 0).start()
+            s2(g, o, 1).wait()
+            G[g][j, y, :, c, hi] = G[g][j, y, :, c, hi] + R[g][j, 0, :, 1, hi]
+            s3(g, o, 1).start()
+
+    def s2_kind_finish(late):
         for h in range(2):
-            s2(g, i, h).start()
-
-    def s1_finish(g, i):
-        s1(g, i).wait()
-        add_s1(g, i)
-
-    def s2_finish(g, i):
-        j = slab(i + 1)
-        s2(g, i, 0).wait()
-        G[g][j, :, x, c, lo] = G[g][j, :, x, c, lo] + R[g][j, 0, :, 1, lo]
-        s3(g, i, 0).start()
-        s2(g, i, 1).wait()
-        G[g][j, y, :, c, hi] = G[g][j, y, :, c, hi] + R[g][j, 0, :, 1, hi]
-        s3(g, i, 1).start()
-
-    def s3_finish(g, i):
-        j = slab(i + 1)
-        s3(g, i, 0).wait()
-        s3(g, i, 1).wait()
-        G[g][j, y, x, c] = G[g][j, y, x, c] + R[g][j, 1, 0, 1]
-        if i < T - 1:
-            sz(g, i).start()
+            s2_kind(late, h).wait()
+        k = 1 - x if late else x
+        G[0][:, k, x, c, lo] = G[0][:, k, x, c, lo] + R[0][:, 0, k, 1, lo]
+        k = 1 - y if late else y
+        G[0][:, y, k, c, hi] = G[0][:, y, k, c, hi] + R[0][:, 0, k, 1, hi]
+
+    def s3_finish(o, *groups):
+        j = slabs[o]
+        for g in groups:
+            s3(g, o, 0).wait()
+            s3(g, o, 1).wait()
+            G[g][j, y, x, c] = G[g][j, y, x, c] + R[g][j, 1, 0, 1]
+            if o:
+                sz_slab(g, o).start()
 
     def f_at(g):
         return G[g].at[:, :, :, 1 - c]
@@ -419,9 +489,9 @@
 
     def z_finish(g):
         total = G[g][z, y, x, c].astype(F32)
-        for i in range(T - 1):
-            sz(g, i).wait()
-            total = total + R[g][i, 1, 1, 1].astype(F32)
+        for o in others:
+            sz(g, o).wait()
+            total = total + R[g][o - 1, 1, 1, 1].astype(F32)
         mine = f_at(g).at[c, y, x]
         mine[...] = total.astype(BF)
         for k in range(3, bits):
@@ -455,8 +525,8 @@
         for k in range(2):
             out_copy(g, k).start()
 
-    def feed(i):
-        j = slab(i + 1)
+    def feed(o, between, after_part, after_down):
+        j = slabs[o]
         up, down = W1.at[j], W2.at[j]
 
         def part(r):
@@ -472,27 +542,70 @@
                 gh[r, :, cols] = (ga * slope).astype(BF)
             gin_ref[r] += nn(act[r], mat(down))
             gn2[r] += nt(gh[r], mat(up))
+            pl.when(r == 0)(between)
 
         loop(rows, part)
+        after_part()
         for m in range(2):
             cols = pl.ds(m * (depth // 2), depth // 2)
             d = tn(act[:, :, cols].reshape(rows * tile, depth // 2), cot_ref[...].reshape(rows * tile, depth))
             G2[j, m] = d.astype(BF).reshape(2, 2, piece, depth)
+        s1(2, o).start()
+        after_down()
+        for m in range(2):
+            cols = pl.ds(m * (depth // 2), depth // 2)
             d = tn(n2[:, :, cols].reshape(rows * tile, depth // 2), gh[...].reshape(rows * tile, depth))
             G1[j, m] = d.astype(BF).reshape(2, 2, piece, depth)
-        s1(1, i).start()
-        s1(2, i).start()
-
-        @pl.when(i > 0)
-        def _():
-            s1_finish(1, i - 1)
-            s1_finish(2, i - 1)
-
-    loop(T, feed)
+        s1(1, o).start()
+
+    def nothing():
+        return
+
+    def own_between():
+        to_2(2, 1, 2)
+        to_3(1, 1, 2)
+
+    def own_part():
+        to_1(3, 1, 2)
+        to_3(2, 1, 2)
+
+    def own_down():
+        to_2(3, 1, 2)
+
+    feed(0, own_between, own_part, own_down)
+    arrived(1, 1, 2)
+
+    def second_between():
+        s1_finish(0, 2, 1)
+
+    def second_part():
+        to_3(3, 1, 2)
+
+    feed(1, second_between, second_part, nothing)
+    arrived(2, 1, 2)
+
+    def third_between():
+        s1_finish(1, 2, 1)
+
+    def third_part():
+        s2_finish(0, 2, 1)
+
+    feed(2, third_between, third_part, nothing)
+    arrived(3, 1, 2)
+    z_sent(0, 1, 2)
+
+    def fourth_between():
+        s1_finish(2, 2, 1)
+
+    def fourth_part():
+        s2_finish(1, 2, 1)
+
+    def fourth_down():
+        s3_finish(0, 2, 1)
+
+    feed(3, fourth_between, fourth_part, fourth_down)
     for dev in partners:
         pl.semaphore_signal(ready, inc=1, device_id=dev, device_id_type=MESH)
-    s1_finish(1, T - 1)
-    s1_finish(2, T - 1)
 
     def norm_two_back(r, carry):
         mixed_ref[r] = gin_ref[r].astype(BF)
@@ -508,9 +621,7 @@
 
     gain2_grad = lax.fori_loop(0, rows, norm_two_back, jnp.zeros((1, depth), F32))
 
-    for i in range(T):
-        s2_finish(1, i)
-        s2_finish(2, i)
+    s1_finish(3, 2, 1)
     pl.semaphore_wait(ready, len(partners))
 
     local[3].start()
@@ -526,6 +637,7 @@
 
     flat = (rows * tile, depth)
     kind(1, 1, mix, 0, n2[...].reshape(flat))
+    s2_finish(2, 2, 1)
 
     def mixer_back(r):
         gmix = nt(n2[r], mat(Wo))
@@ -540,10 +652,11 @@
     loop(rows, mixer_back)
     cs_start(1, nn(ones, gs[0]), nn(ones, gs[1]))
     kind(0, 0, act, 0, n1[:, 1].reshape(flat))
-
-    for i in range(T):
-        s3_finish(1, i)
-        s3_finish(2, i)
+    s3_finish(1, 2, 1)
+    s1_kind_finish(1, 1)
+    s1_kind_finish(0, 0)
+    for h in range(2):
+        s2_kind(0, h).start()
 
     local[3].wait()
     gband = nt(gs[0], pairs[0].reshape(3 * tile, 2 * depth)) + nt(gs[1], pairs[1].reshape(3 * tile, 2 * depth))
@@ -583,8 +696,7 @@
         return rc(ref, ref, p_base + 5, core)
 
     p1().start()
-    z_finish(1)
-    z_finish(2)
+    s2_finish(3, 2, 1)
     cs_finish(1)
 
     def pairs_back(r):
@@ -600,24 +712,23 @@
             pairs[r, t, :, pl.ds(0, depth)] = (gn * wv + gd * we).astype(BF)
             pairs[r, t, :, pl.ds(depth, depth)] = (gn * we).astype(BF)
 
-    loop(rows, pairs_back)
+    pairs_back(0)
+    s3_finish(2, 2, 1)
+    pairs_back(1)
     p1().wait()
     GP[:, :, c] = GP[:, :, c] + RP[:, :, 0]
     p2().start()
-
     n1_all = n1[...].reshape(3 * rows * tile, depth)
     kind(0, 1, pairs, 0, n1_all)
-    f1_finish(1)
-    f1_finish(2)
+    s3_finish(3, 2, 1)
     kind(1, 0, pairs, depth, n1_all)
+    s1_kind_finish(0, 1)
+    s1_kind_finish(1, 0)
+    for h in range(2):
+        s2_kind(1, h).start()
     p2().wait()
     GP[:, x, c] = GP[:, x, c] + RP[0, :, 1]
     p3().start()
-    for ty in range(2):
-        for tx in range(2):
-            s1_kind(ty, tx).wait()
-    for i in range(T):
-        add_s1(0, i)
 
     def halo_part(d):
         def body(r):
@@ -628,17 +739,22 @@
         loop(rows, body)
 
     def back_left():
-        return rc(gs.at[:, :, pl.ds(0, depth)], hr.at[1], halo_base + 2, (b, lax.max(z - 1, 0)))
+        return rc(gs.at[:, :, pl.ds(0, depth)], hr.at[1], halo_base, left)
 
     def back_right():
-        return rc(gs.at[:, :, pl.ds(depth, depth)], hr.at[0], halo_base + 3, (b, lax.min(z + 1, T - 1)))
+        return rc(gs.at[:, :, pl.ds(depth, depth)], hr.at[0], halo_base + 1, right)
 
     halo_part(0)
     pl.when(z > 0)(lambda: back_left().start())
     halo_part(1)
     pl.when(z < T - 1)(lambda: back_right().start())
-    for i in range(T):
-        s2_finish(0, i)
+    s2_kind_finish(0)
+    s2_kind_finish(1)
+    for o in (1, 2, 3, 0):
+        for h in range(2):
+            s3(0, o, h).start()
+    z_finish(2)
+    z_finish(1)
 
     def own_grad(r):
         g = nn(act[r], mat(Wq)) + nn(pairs[r, 1, :, pl.ds(0, depth)], mat(Wk))
@@ -646,8 +762,8 @@
 
     loop(rows, own_grad)
     x_again.start()
-    f2_finish(1)
-    f2_finish(2)
+    f1_finish(2)
+    f1_finish(1)
     p3().wait()
     GP[y, x, c] = GP[y, x, c] + RP[1, 0, 1]
     for k in range(3, bits):
@@ -658,8 +774,10 @@
     FP[z, y, x, c] = GP[y, x, c]
     for i in others:
         pz(i).start()
-    for i in range(T):
-        s3_finish(0, i)
+    for o in (1, 2, 3, 0):
+        s3_finish(o, 0)
+    f2_finish(2)
+    f2_finish(1)
 
     pl.when(z > 0)(lambda: back_left().wait_send())
     pl.when(z < T - 1)(lambda: back_right().wait_send())

time: 239 us -> 205 us (0.86); the launches traced: 234 us -> 203 us
  Pallas kernels: 213 us -> 182 us
    pallas_call x1, Pallas kernels: 213 us -> 182 us  [per_device(): pl.pallas_call(functools.partial(kernel, T, bits, T * tile, n_sems), out_...]
where the time goes in v2:
time: 205 us; the launch traced here: 203 us
  Pallas kernels  182 us (89%)
  local copies, waits for them, and re-layouts  17 us (8%)
  other arithmetic  3.64 us (2%)
    pallas_call x1, Pallas kernels, per_device(): pl.pallas_call(functools.partial(kernel, T, bits, T * tile, n_sems), out_...  182 us
    unnamed x14, local copies, waits for them, and re-layouts  6.76 us

profile of v2, /device:TPU:0, one launch (start us, length us, event | category | flops | bytes accessed | tf_op | source)
XLA Modules:
  0.0 203.1 jit_solution(14919344230985575437)
XLA Ops:
  0.6 0.0 copy-start.4
  0.7 0.0 copy-start.5
  0.7 0.0 copy-start.3
  0.7 0.0 copy-start.2
  0.7 2.8 %copy_bitcast_fusion = (bf16[2,256,768]{2,1,0:T(8,128)(2,1)}, bf16[2,256,768]{2,1,0:T(8,128)(2,1)}) fusion(bf16[256,2,768]{2,1,0:T(2,128)(2,1)} %param.19, bf16[256,2,768]{2,1,0:T(2,128)(2,1)} %param.10), kind=kLoop, calls=%fused_computation.2 | loop fusion | bytes 3145728 | tf_op jit(solution)/shard_map/transpose | solution.py:873
  3.5 0.0 copy-done.4
  3.5 0.6 reshape.42.gain1_ref
  4.1 0.0 copy-done.5
  4.1 0.6 reshape.43.gain2_ref
  4.7 0.0 copy-done.3
  4.7 0.0 copy-done.2
  4.7 1.1 pad_maximum_fusion
  5.8 181.7 %shard_map.169 = (bf16[2,256,768]{2,1,0:T(8,128)(2,1)}, f32[2,256,768]{2,1,0:T(8,128)}, f32[8,768]{1,0:T(8,128)}, bf16[3,2,2,2,96,768]{5,4,3,2,1,0:T(8,128)(2,1)}, bf16[4,2,2,2,32,512]{5,4,3,2,1,0:T(8,128)(2,1)}) custom-call(s32[2]{0:T(128)} %len_ref.1, bf16[2,256,768]{2,1,0:T(8,128)(2,1)} %get-tuple-element.33.x_ref, ...), custom_call_target="tpu_custom_call" | custom-call | tf_op jit(solution)/shard_map/pallas_call | solution.py:921
  187.5 0.0 copy-start
  187.5 3.0 %copy.21 = bf16[256,2,768]{2,1,0:T(2,128)(2,1)} copy(bf16[256,2,768]{2,0,1:T(8,128)(2,1)} %bitcast.32) | data formatting | bytes 1572864
  190.5 3.8 %copy.22 = f32[256,2,768]{2,1,0:T(2,128)} copy(f32[256,2,768]{2,0,1:T(8,128)} %bitcast.28) | data formatting | bytes 3145728
  194.2 1.4 slice_reduce_fusion
  195.7 0.0 copy-done
  195.7 0.8 convert_element_type.14
  196.5 1.3 slice.34
  197.9 0.9 slice_bitcast_fusion
  198.7 0.0 copy-start.1
  198.7 2.7 %fusion = (f32[1,2,2,2,96,768]{5,4,3,2,1,0:T(8,128)}, f32[1,2,2,2,96,768]{5,4,3,2,1,0:T(8,128)}) fusion(bf16[3,2,2,2,96,768]{5,4,3,2,1,0:T(8,128)(2,1)S(1)} %copy-done), kind=kLoop, calls=%fused_computation.7 | loop fusion | bytes 9437184 | tf_op jit(solution)/shard_map/slice | solution.py:957
  201.4 0.0 copy-done.1
  201.4 1.7 bitcast_convert_fusion
Async XLA Ops:
  0.6 2.8 %copy-start.4 = (bf16[768]{0:T(1024)(128)(2,1)S(1)}, bf16[768]{0:T(1024)(128)(2,1)}, u32[]{:S(2)}) copy-start(bf16[768]{0:T(1024)(128)(2,1)} %param.12) | copy-start | bytes 4612
  0.7 3.4 %copy-start.5 = (bf16[768]{0:T(1024)(128)(2,1)S(1)}, bf16[768]{0:T(1024)(128)(2,1)}, u32[]{:S(2)}) copy-start(bf16[768]{0:T(1024)(128)(2,1)} %param.15) | copy-start | bytes 4612
  0.7 4.0 %copy-start.3 = (bf16[192,768]{1,0:T(8,128)(2,1)S(1)}, bf16[192,768]{1,0:T(8,128)(2,1)}, u32[]{:S(2)}) copy-start(bf16[192,768]{1,0:T(8,128)(2,1)} %param.14) | copy-start | bytes 884740
  0.7 4.0 %copy-start.2 = (bf16[3,768,192]{1,2,0:T(8,128)(2,1)S(1)}, bf16[3,768,192]{1,2,0:T(8,128)(2,1)}, u32[]{:S(2)}) copy-start(bf16[3,768,192]{1,2,0:T(8,128)(2,1)} %param.13) | copy-start | bytes 2654212
  187.5 8.2 %copy-start = (bf16[3,2,2,2,96,768]{5,4,3,2,1,0:T(8,128)(2,1)S(1)}, bf16[3,2,2,2,96,768]{5,4,3,2,1,0:T(8,128)(2,1)}, u32[]{:S(2)}) copy-start(bf16[3,2,2,2,96,768]{5,4,3,2,1,0:T(8,128)(2,1)} %get-tuple-element.17) | copy-start | bytes 10616836
  198.7 2.7 %copy-start.1 = (bf16[4,2,2,2,32,512]{5,4,3,2,1,0:T(8,128)(2,1)S(1)}, bf16[4,2,2,2,32,512]{5,4,3,2,1,0:T(8,128)(2,1)}, u32[]{:S(2)}) copy-start(bf16[4,2,2,2,32,512]{5,4,3,2,1,0:T(8,128)(2,1)} %get-tuple-element.18) | copy-start | bytes 3145732

commit v3 on v2

--- a/solution.py
+++ b/solution.py
@@ -45,16 +45,19 @@
     len_ref,
     x_ref,
     cot_ref,
-    gain1_ref,
-    gain2_ref,
+    gain_ref,
     w0_in,
     w1_in,
     w2_in,
     bias_in,
     mixed_ref,
     gin_ref,
-    gains_ref,
-    f_out,
+    gains1_ref,
+    gains2_ref,
+    fq_out,
+    fo_out,
+    f1_out,
+    f2_out,
     fp_out,
     W0,
     W1,
@@ -254,12 +257,14 @@
         n1[:, 2] = jnp.zeros((rows, tile, depth), BF)
         hr[1] = jnp.zeros((rows, tile, depth), BF)
 
-    gain1 = gain1_ref[...]
-    gain2 = gain2_ref[...]
-
-    def loop(n, body):
+    gain1 = gain_ref[0:1]
+    gain2 = gain_ref[1:2]
+
+    def loop(n, body, between=None):
         def step(i, carry):
             body(i)
+            if between is not None:
+                pl.when(i == 0)(between)
             return carry
 
         lax.fori_loop(0, n, step, 0)
@@ -279,22 +284,42 @@
 
     Wq, Wk, Wv, Wo = W0.at[0, 0], W0.at[0, 1], W0.at[1, 0], W0.at[1, 1]
 
-    to_1(1, 0)
-    to_1(2, 0)
-
     def halo_start():
         for r in range(rows):
             pl.when(has_right)(lambda: halo_right(r).start())
             pl.when(has_left)(lambda: halo_left(r).start())
 
+    at_end = (z == 0) | (z == T - 1)
+
+    inside = z * (T - 1 - z) > 0
+
+    def ends(step, *args):
+        pl.when(at_end)(lambda: step(*args))
+
+    def middles(step, *args):
+        pl.when(inside)(lambda: step(*args))
+
+    @pl.when(at_end)
+    def _():
+        z_start(2, 1)
+        halo_start()
+
+    to_1(1, 0)
+    to_1(2, 0)
     to_2(1, 0)
     to_1(3, 0)
-    halo_start()
-    z_start(1, 2)
+
+    @pl.when(inside)
+    def _():
+        z_start(2, 1)
+        halo_start()
+
     to_2(2, 0)
     to_3(1, 0)
     to_2(3, 0)
     to_3(2, 0)
+    to_1(1, 2, 1)
+    middles(to_1, 2, 2, 1)
     to_3(3, 0)
     for k in others:
         arrived(k, 0)
@@ -313,7 +338,8 @@
         gates[r] = jax.nn.sigmoid(nt(n1[r, 1], mat(Wq)))
         key_values(r, 1)
 
-    loop(rows, own_qkv)
+    loop(rows, own_qkv, lambda: to_2(1, 2, 1))
+    middles(to_2, 2, 2, 1)
 
     ones = jnp.ones((8, tile), BF)
     row_of = lax.broadcasted_iota(jnp.int32, (8, 1), 0)
@@ -353,7 +379,7 @@
             key_values(r, t)
 
     loop(rows, halo_kv)
-    to_1(1, 1, 2)
+    to_3(1, 2, 1)
     cs_finish(0)
 
     x_again = pltpu.make_async_copy(x_ref, act, lsem.at[4])
@@ -369,10 +395,8 @@
         ratio[r] = rt
         mix[r] = (gates[r] * rt).astype(BF)
 
-    mixer(0)
-    to_1(2, 1, 2)
-    mixer(1)
-    to_2(1, 1, 2)
+    loop(rows, mixer, lambda: middles(to_3, 2, 2, 1))
+    ends(to_1, 2, 2, 1)
     x_again.wait()
 
     def middle(r):
@@ -390,6 +414,7 @@
     G = (W1, G1, G2)
     R = (W2, R1, R2)
     s1_base, s2_base, s3_base, sz_base, f_base = take(12), take(24), take(24), take(3 * T), take(15)
+    early_base = take(2)
     def s1(g, o):
         j = slabs[o]
         return rc(G[g].at[j, :, :, 1 - c], R[g].at[j, :, :, 0], s1_base + g * 4 + o, core)
@@ -405,14 +430,20 @@
             src, dst, dev = G[g].at[j, 1 - y, :, c, hi], R[g].at[j, 0, :, 1, hi], yp
         return rc(src, dst, s2_base + (g * 2 + h) * 4 + o, dev)
 
-    def s2_kind(late, h):
+    def s2_early(h):
         if h == 0:
-            k = x if late else 1 - x
-            src, dst, dev = G[0].at[:, k, 1 - x, c, lo], R[0].at[:, 0, k, 1, lo], xp
+            src, dst, dev = G[0].at[:, 1 - x, 1 - x, c, lo], R[0].at[:, 0, 1 - x, 1, lo], xp
         else:
-            k = y if late else 1 - y
-            src, dst, dev = G[0].at[:, 1 - y, k, c, hi], R[0].at[:, 0, k, 1, hi], yp
-        return rc(src, dst, s2_base + h * 4 + late, dev)
+            src, dst, dev = G[0].at[:, 1 - y, 1 - y, c, hi], R[0].at[:, 0, 1 - y, 1, hi], yp
+        return rc(src, dst, early_base + h, dev)
+
+    def s2_late(o, h):
+        j = slabs[o]
+        if h == 0:
+            src, dst, dev = G[0].at[j, x, 1 - x, c, lo], R[0].at[j, 0, x, 1, lo], xp
+        else:
+            src, dst, dev = G[0].at[j, 1 - y, y, c, hi], R[0].at[j, 0, y, 1, hi], yp
+        return rc(src, dst, s2_base + h * 4 + o, dev)
 
     def s3(g, o, h):
         j = slabs[o]
@@ -422,14 +453,15 @@
             src, dst, dev = G[g].at[j, y, 1 - x, c, hi], R[g].at[j, 1, 0, 1, hi], xp
         return rc(src, dst, s3_base + (g * 2 + h) * 4 + o, dev)
 
-    def sz(g, o):
-        j = lax.rem(z - o + T, T)
-        return rc(G[g].at[j, y, x, c], R[g].at[o - 1, 1, 1, 1], sz_base + g * T + o, (b, j))
-
-    def sz_slab(g, k):
-        j = slabs[k]
-        o = lax.rem(z - j + T, T)
-        return rc(G[g].at[j, y, x, c], R[g].at[o - 1, 1, 1, 1], sz_base + g * T + o, (b, j))
+    pair = z + 1 - 2 * lax.rem(z, 2)
+    across = lax.rem(z + 2, T)
+
+    def sz_1(g, slot):
+        j = lax.rem(pair + 2 * slot, T)
+        return rc(G[g].at[j, y, x, c], R[g].at[slot, 1, 1, 1], sz_base + g * T + slot, (b, pair))
+
+    def sz_2(g):
+        return rc(G[g].at[across, y, x, c], R[g].at[2, 1, 1, 1], sz_base + g * T + 2, (b, across))
 
     def s1_finish(o, *groups):
         j = slabs[o]
@@ -453,13 +485,30 @@
             G[g][j, y, :, c, hi] = G[g][j, y, :, c, hi] + R[g][j, 0, :, 1, hi]
             s3(g, o, 1).start()
 
-    def s2_kind_finish(late):
+    last_order = (1, 2, 3, 0)
+
+    def s3_start(o):
         for h in range(2):
-            s2_kind(late, h).wait()
-        k = 1 - x if late else x
-        G[0][:, k, x, c, lo] = G[0][:, k, x, c, lo] + R[0][:, 0, k, 1, lo]
-        k = 1 - y if late else y
-        G[0][:, y, k, c, hi] = G[0][:, y, k, c, hi] + R[0][:, 0, k, 1, hi]
+            s3(0, o, h).start()
+
+    def s2_early_finish():
+        for h in range(2):
+            s2_early(h).wait()
+        G[0][:, x, x, c, lo] = G[0][:, x, x, c, lo] + R[0][:, 0, x, 1, lo]
+        G[0][:, y, y, c, hi] = G[0][:, y, y, c, hi] + R[0][:, 0, y, 1, hi]
+
+        @pl.when(x != y)
+        def _():
+            for o in last_order:
+                s3_start(o)
+
+    def s2_late_finish(o):
+        j = slabs[o]
+        for h in range(2):
+            s2_late(o, h).wait()
+        G[0][j, 1 - x, x, c, lo] = G[0][j, 1 - x, x, c, lo] + R[0][j, 0, 1 - x, 1, lo]
+        G[0][j, y, 1 - y, c, hi] = G[0][j, y, 1 - y, c, hi] + R[0][j, 0, 1 - y, 1, hi]
+        pl.when(x == y)(lambda: s3_start(o))
 
     def s3_finish(o, *groups):
         j = slabs[o]
@@ -467,8 +516,9 @@
             s3(g, o, 0).wait()
             s3(g, o, 1).wait()
             G[g][j, y, x, c] = G[g][j, y, x, c] + R[g][j, 1, 0, 1]
-            if o:
-                sz_slab(g, o).start()
+            for slot in range(2):
+                if o:
+                    pl.when(j == lax.rem(pair + 2 * slot, T))(lambda: sz_1(g, slot).start())
 
     def f_at(g):
         return G[g].at[:, :, :, 1 - c]
@@ -487,11 +537,15 @@
 
     u_base = take(4 * max(bits - 3, 0))
 
+    def z_middle(g):
+        sz_1(g, 1).wait()
+        G[g][across, y, x, c] = G[g][across, y, x, c] + R[g][1, 1, 1, 1]
+        sz_2(g).start()
+
     def z_finish(g):
-        total = G[g][z, y, x, c].astype(F32)
-        for o in others:
-            sz(g, o).wait()
-            total = total + R[g][o - 1, 1, 1, 1].astype(F32)
+        sz_1(g, 0).wait()
+        sz_2(g).wait()
+        total = G[g][z, y, x, c].astype(F32) + R[g][0, 1, 1, 1].astype(F32) + R[g][2, 1, 1, 1].astype(F32)
         mine = f_at(g).at[c, y, x]
         mine[...] = total.astype(BF)
         for k in range(3, bits):
@@ -516,16 +570,25 @@
             f2(g, h).wait()
         f3(g).start()
 
-    def out_copy(g, k):
-        src = G[g].at[k, :, :, 1 - c]
-        return pltpu.make_async_copy(src, f_out.at[g, :, :, k], lsem.at[5 + 2 * g + k])
+    def out_copies(g):
+        pairs_of = []
+        for k in range(2):
+            if g:
+                pairs_of.append((G[g].at[k, :, :, 1 - c], (f1_out, f2_out)[g - 1].at[:, :, k]))
+                continue
+            for ty in range(2):
+                for tx in range(2):
+                    dst = fo_out.at[k] if ty + tx == 2 else fq_out.at[2 * ty + tx, k]
+                    pairs_of.append((G[0].at[k, ty, tx, 1 - c], dst))
+        first = (5, 13, 15)[g]
+        return [pltpu.make_async_copy(src, dst, lsem.at[first + i]) for i, (src, dst) in enumerate(pairs_of)]
 
     def f3_finish(g):
         f3(g).wait()
-        for k in range(2):
-            out_copy(g, k).start()
-
-    def feed(o, between, after_part, after_down):
+        for cp in out_copies(g):
+            cp.start()
+
+    def feed(o, between, after_sums):
         j = slabs[o]
         up, down = W1.at[j], W2.at[j]
 
@@ -540,70 +603,43 @@
                 act[r, :, cols] = (hh + hh * t).astype(BF)
                 slope = 0.5 + 0.5 * t + hh * (1.0 - t * t) * (GELU_C + (3.0 * GELU_C * GELU_A) * sq)
                 gh[r, :, cols] = (ga * slope).astype(BF)
+
+        def collect(r):
             gin_ref[r] += nn(act[r], mat(down))
             gn2[r] += nt(gh[r], mat(up))
-            pl.when(r == 0)(between)
-
-        loop(rows, part)
-        after_part()
-        for m in range(2):
-            cols = pl.ds(m * (depth // 2), depth // 2)
-            d = tn(act[:, :, cols].reshape(rows * tile, depth // 2), cot_ref[...].reshape(rows * tile, depth))
-            G2[j, m] = d.astype(BF).reshape(2, 2, piece, depth)
-        s1(2, o).start()
-        after_down()
-        for m in range(2):
-            cols = pl.ds(m * (depth // 2), depth // 2)
-            d = tn(n2[:, :, cols].reshape(rows * tile, depth // 2), gh[...].reshape(rows * tile, depth))
-            G1[j, m] = d.astype(BF).reshape(2, 2, piece, depth)
-        s1(1, o).start()
+
+        loop(rows, part, between)
+        for g, lhs, rhs in ((2, act, cot_ref), (1, n2, gh)):
+            for m in range(2):
+                cols = pl.ds(m * (depth // 2), depth // 2)
+                d = tn(lhs[:, :, cols].reshape(rows * tile, depth // 2), rhs[...].reshape(rows * tile, depth))
+                G[g][j, m] = d.astype(BF).reshape(2, 2, piece, depth)
+            s1(g, o).start()
+        after_sums()
+        loop(rows, collect)
+        s1_finish(o, 2, 1)
 
     def nothing():
         return
 
-    def own_between():
-        to_2(2, 1, 2)
-        to_3(1, 1, 2)
-
-    def own_part():
-        to_1(3, 1, 2)
-        to_3(2, 1, 2)
-
-    def own_down():
-        to_2(3, 1, 2)
-
-    feed(0, own_between, own_part, own_down)
-    arrived(1, 1, 2)
+    feed(0, lambda: middles(to_1, 3, 2, 1), lambda: ends(to_2, 2, 2, 1))
+    arrived(1, 2, 1)
 
     def second_between():
-        s1_finish(0, 2, 1)
-
-    def second_part():
-        to_3(3, 1, 2)
-
-    feed(1, second_between, second_part, nothing)
-    arrived(2, 1, 2)
-
-    def third_between():
-        s1_finish(1, 2, 1)
-
-    def third_part():
-        s2_finish(0, 2, 1)
-
-    feed(2, third_between, third_part, nothing)
-    arrived(3, 1, 2)
+        middles(to_2, 3, 2, 1)
+        ends(to_3, 2, 2, 1)
+        ends(to_1, 3, 2, 1)
+
+    def second_sums():
+        middles(to_3, 3, 2, 1)
+        ends(to_2, 3, 2, 1)
+
+    feed(1, second_between, second_sums)
+    arrived(2, 2, 1)
+    feed(2, lambda: ends(to_3, 3, 2, 1), nothing)
+    arrived(3, 2, 1)
     z_sent(0, 1, 2)
-
-    def fourth_between():
-        s1_finish(2, 2, 1)
-
-    def fourth_part():
-        s2_finish(1, 2, 1)
-
-    def fourth_down():
-        s3_finish(0, 2, 1)
-
-    feed(3, fourth_between, fourth_part, fourth_down)
+    feed(3, lambda: s2_finish(1, 2, 1), nothing)
     for dev in partners:
         pl.semaphore_signal(ready, inc=1, device_id=dev, device_id_type=MESH)
 
@@ -621,7 +657,7 @@
 
     gain2_grad = lax.fori_loop(0, rows, norm_two_back, jnp.zeros((1, depth), F32))
 
-    s1_finish(3, 2, 1)
+    s2_finish(2, 2, 1)
     pl.semaphore_wait(ready, len(partners))
 
     local[3].start()
@@ -637,7 +673,7 @@
 
     flat = (rows * tile, depth)
     kind(1, 1, mix, 0, n2[...].reshape(flat))
-    s2_finish(2, 2, 1)
+    s3_finish(1, 2, 1)
 
     def mixer_back(r):
         gmix = nt(n2[r], mat(Wo))
@@ -651,12 +687,9 @@
 
     loop(rows, mixer_back)
     cs_start(1, nn(ones, gs[0]), nn(ones, gs[1]))
+    s2_finish(3, 2, 1)
     kind(0, 0, act, 0, n1[:, 1].reshape(flat))
-    s3_finish(1, 2, 1)
-    s1_kind_finish(1, 1)
-    s1_kind_finish(0, 0)
-    for h in range(2):
-        s2_kind(0, h).start()
+    s3_finish(2, 2, 1)
 
     local[3].wait()
     gband = nt(gs[0], pairs[0].reshape(3 * tile, 2 * depth)) + nt(gs[1], pairs[1].reshape(3 * tile, 2 * depth))
@@ -696,7 +729,10 @@
         return rc(ref, ref, p_base + 5, core)
 
     p1().start()
-    s2_finish(3, 2, 1)
+    s1_kind_finish(1, 1)
+    s1_kind_finish(0, 0)
+    for h in range(2):
+        s2_early(h).start()
     cs_finish(1)
 
     def pairs_back(r):
@@ -712,23 +748,17 @@
             pairs[r, t, :, pl.ds(0, depth)] = (gn * wv + gd * we).astype(BF)
             pairs[r, t, :, pl.ds(depth, depth)] = (gn * we).astype(BF)
 
-    pairs_back(0)
-    s3_finish(2, 2, 1)
-    pairs_back(1)
+    loop(rows, pairs_back, lambda: s3_finish(3, 2, 1))
     p1().wait()
     GP[:, :, c] = GP[:, :, c] + RP[:, :, 0]
     p2().start()
     n1_all = n1[...].reshape(3 * rows * tile, depth)
     kind(0, 1, pairs, 0, n1_all)
-    s3_finish(3, 2, 1)
+    s2_finish(0, 2, 1)
+    z_middle(2)
+    z_middle(1)
     kind(1, 0, pairs, depth, n1_all)
     s1_kind_finish(0, 1)
-    s1_kind_finish(1, 0)
-    for h in range(2):
-        s2_kind(1, h).start()
-    p2().wait()
-    GP[:, x, c] = GP[:, x, c] + RP[0, :, 1]
-    p3().start()
 
     def halo_part(d):
         def body(r):
@@ -745,16 +775,18 @@
         return rc(gs.at[:, :, pl.ds(depth, depth)], hr.at[0], halo_base + 1, right)
 
     halo_part(0)
-    pl.when(z > 0)(lambda: back_left().start())
+    pl.when(has_left)(lambda: back_left().start())
+    s1_kind_finish(1, 0)
+    for o in last_order:
+        for h in range(2):
+            s2_late(o, h).start()
     halo_part(1)
-    pl.when(z < T - 1)(lambda: back_right().start())
-    s2_kind_finish(0)
-    s2_kind_finish(1)
-    for o in (1, 2, 3, 0):
-        for h in range(2):
-            s3(0, o, h).start()
-    z_finish(2)
-    z_finish(1)
+    pl.when(has_right)(lambda: back_right().start())
+    p2().wait()
+    GP[:, x, c] = GP[:, x, c] + RP[0, :, 1]
+    p3().start()
+    s2_early_finish()
+    s3_finish(0, 2, 1)
 
     def own_grad(r):
         g = nn(act[r], mat(Wq)) + nn(pairs[r, 1, :, pl.ds(0, depth)], mat(Wk))
@@ -762,8 +794,8 @@
 
     loop(rows, own_grad)
     x_again.start()
-    f1_finish(2)
-    f1_finish(1)
+    for o in last_order:
+        s2_late_finish(o)
     p3().wait()
     GP[y, x, c] = GP[y, x, c] + RP[1, 0, 1]
     for k in range(3, bits):
@@ -774,10 +806,18 @@
     FP[z, y, x, c] = GP[y, x, c]
     for i in others:
         pz(i).start()
-    for o in (1, 2, 3, 0):
+    z_finish(2)
+    z_finish(1)
+    for i in others:
+        pz(i).wait()
+    pa1().start()
+    for o in last_order:
         s3_finish(o, 0)
-    f2_finish(2)
-    f2_finish(1)
+    f1_finish(2)
+    f1_finish(1)
+    z_middle(0)
+    pa1().wait()
+    pa2().start()
 
     pl.when(z > 0)(lambda: back_left().wait_send())
     pl.when(z < T - 1)(lambda: back_right().wait_send())
@@ -816,36 +856,34 @@
                 gz(i).start()
 
     ga(0).start()
-    f3_finish(1)
-    f3_finish(2)
+    f2_finish(2)
+    f2_finish(1)
     gains_step(0)
-    for i in others:
-        pz(i).wait()
-    pa1().start()
+    z_finish(0)
+    pa2().wait()
+    pa3().start()
     gains_step(1)
-    z_finish(0)
+    f1_finish(0)
     gains_step(2)
     for k in range(3, bits):
         gains_step(k)
-    pa1().wait()
-    pa2().start()
-    f1_finish(0)
+    f3_finish(2)
+    f3_finish(1)
+    f2_finish(0)
     for i in others:
         gz(i).wait()
     total = GR[bits]
     for i in range(1, T):
         total = total + GR[bits + i]
-    gains_ref[...] = total
-    pa2().wait()
-    pa3().start()
-    f2_finish(0)
+    gains1_ref[...] = total[0:1]
+    gains2_ref[...] = total[1:2]
     pa3().wait()
     fp_copy = pltpu.make_async_copy(FP, fp_out, lsem.at[3])
     fp_copy.start()
     f3_finish(0)
     for g in range(3):
-        for k in range(2):
-            out_copy(g, k).wait()
+        for cp in out_copies(g):
+            cp.wait()
     fp_copy.wait()
 
 
@@ -914,21 +952,25 @@
         pltpu.VMEM((upper, strip, window), BF),
         pltpu.SemaphoreType.DMA((n_sems,)),
         pltpu.SemaphoreType.DMA((n_sems,)),
-        pltpu.SemaphoreType.DMA((11,)),
+        pltpu.SemaphoreType.DMA((17,)),
         pltpu.SemaphoreType.REGULAR,
         pltpu.SemaphoreType.REGULAR((3, upper)),
     ]
-    mixed, grad_inputs, gains, sums, pair = pl.pallas_call(
+    mixed, grad_inputs, gains1, gains2, fq, fo, f1, f2, pair = pl.pallas_call(
         functools.partial(kernel, T, bits, T * tile, n_sems),
         out_shape=(
             jax.ShapeDtypeStruct(tokens, BF),
             jax.ShapeDtypeStruct(tokens, F32),
-            jax.ShapeDtypeStruct((8, depth), F32),
-            jax.ShapeDtypeStruct((3,) + cut, BF),
+            jax.ShapeDtypeStruct((1, depth), F32),
+            jax.ShapeDtypeStruct((1, depth), F32),
+            jax.ShapeDtypeStruct((3, 2, piece, depth), BF),
+            jax.ShapeDtypeStruct((2, piece, depth), BF),
+            jax.ShapeDtypeStruct(cut, BF),
+            jax.ShapeDtypeStruct(cut, BF),
             jax.ShapeDtypeStruct((T, 2, 2, 2, strip, window), BF),
         ),
-        in_specs=[pl.BlockSpec(memory_space=pltpu.SMEM), hbm, vmem, vmem, vmem, hbm, hbm, hbm, hbm],
-        out_specs=(vmem, vmem, vmem, hbm, hbm),
+        in_specs=[pl.BlockSpec(memory_space=pltpu.SMEM), hbm, vmem, vmem, hbm, hbm, hbm, hbm],
+        out_specs=(vmem, vmem, vmem, vmem, hbm, hbm, hbm, hbm, hbm),
         scratch_shapes=scratch,
         compiler_params=pltpu.CompilerParams(
             collective_id=0, has_side_effects=True, vmem_limit_bytes=VMEM_BYTES
@@ -937,24 +979,22 @@
         lengths,
         x,
         cot,
-        gain_one.astype(F32)[None],
-        gain_two.astype(F32)[None],
+        jnp.stack([gain_one, gain_two]).astype(F32),
         w0,
         w1,
         w2,
         pair_bias,
     )
-    sums = sums.reshape(3, depth, depth).astype(F32)
-    first = sums[0].reshape(4, channels, depth)
+    turned = lax.optimization_barrier(jnp.transpose(fq.reshape(3, channels, depth), (0, 2, 1)))
     return (
         jnp.transpose(mixed, (1, 0, 2)),
         jnp.transpose(grad_inputs, (1, 0, 2)),
-        gains[0],
-        jnp.transpose(first[:3], (0, 2, 1)),
-        first[3],
-        gains[1],
-        sums[1],
-        sums[2],
+        gains1.reshape(depth),
+        turned.astype(F32),
+        fo.reshape(channels, depth).astype(F32),
+        gains2.reshape(depth),
+        f1.reshape(depth, depth).astype(F32),
+        f2.reshape(depth, depth).astype(F32),
         pair.reshape(T * tile, window).astype(F32),
     )
 

time: 205 us -> 202 us (0.985)
  local copies, waits for them, and re-layouts: 17 us -> 6.7 us
  other arithmetic: 3.64 us -> 12.5 us
    convert_element_type x1 -> x4, other arithmetic: 0.84 us -> 7.09 us  [the longest x1 4.26 us: per_device(): f2.reshape(depth, depth).astype(F32)]
    slice x3 -> x0, local copies, waits for them, and re-layouts: 5.44 us -> none  [the longest x1 2.69 us: per_device(): sums[2]]
    transpose x1 -> x0, local copies, waits for them, and re-layouts: 2.8 us -> none  [per_device(): cot = jnp.transpose(cotangent, (1, 0, 2))]
    unnamed x14 -> x26, local copies, waits for them, and re-layouts: 6.76 us -> 6.69 us
where the time goes in v3:
time: 202 us; the launch traced here: 201 us
  Pallas kernels  182 us (90%)
  other arithmetic  12.5 us (6%)
  local copies, waits for them, and re-layouts  6.7 us (3%)
    pallas_call x1, Pallas kernels, per_device(): pl.pallas_call(functools.partial(kernel, T, bits, T * tile, n_sems), out_...  182 us
    unnamed x26, local copies, waits for them, and re-layouts  6.69 us
    convert_element_type x1, other arithmetic, per_device(): f2.reshape(depth, depth).astype(F32)  4.26 us

profile of v3, /device:TPU:0, one launch (start us, length us, event | category | flops | bytes accessed | tf_op | source)
XLA Modules:
  0.0 201.4 jit_solution(6794100856099006614)
XLA Ops:
  0.6 0.0 copy-start.3
  0.7 0.0 copy-start.4
  0.7 2.5 %pad_maximum_fusion = bf16[4,192,768]{2,1,0:T(8,128)(2,1)} fusion(bf16[1,192,768]{2,1,0:T(8,128)(2,1)} %bitcast.37, bf16[3,192,768]{2,1,0:T(8,128)(2,1)} %bitcast.34), kind=kLoop, calls=%fused_computation | loop fusion | flops 589824 | bytes 2359296 | tf_op jit(solution)/shard_map/concatenate | solution.py:913
  3.2 0.0 copy-done.3
  3.2 0.0 copy-start.9
  3.2 0.0 copy-start.10
  3.2 1.0 copy.25
  4.1 0.0 copy-done.4
  4.1 1.0 copy.26
  5.1 0.0 copy-done.9
  5.1 0.0 copy-done.10
  5.1 0.6 maximum_convert_fusion.gain_ref
  5.7 181.5 %shard_map.169 = (bf16[2,256,768]{2,1,0:T(8,128)(2,1)}, f32[2,256,768]{2,1,0:T(8,128)}, f32[1,768]{1,0:T(1,128)}, f32[1,768]{1,0:T(1,128)}, bf16[3,2,96,768]{3,2...) custom-call(s32[2]{0:T(128)} %len_ref.1, ...), custom_call_target="tpu_custom_call" | custom-call | tf_op jit(solution)/shard_map/pallas_call | solution.py:959
  187.2 0.0 copy-start.1
  187.2 4.3 %bitcast_convert_fusion = (f32[768,768]{1,0:T(8,128)}, f32[768,768]{1,0:T(8,128)}) fusion(bf16[2,2,2,96,768]{4,3,2,1,0:T(8,128)(2,1)} %get-tuple-element.25, bf16[2,2,2,96,768]{4,3,2,1,0:T(8,128)(2,1)} %get-tuple-element.24), kind=kLoop, calls=%fused_computation.1 | loop fusion | flops 1179648 | bytes 7077888 | tf_op jit(solution)/shard_map/convert_element_type | solution.py:997
  191.5 0.0 copy-done.1
  191.5 0.0 copy-start.2
  191.5 1.7 bitcast_convert_fusion.2
  193.2 0.0 copy-start
  193.2 0.0 copy-done.2
  193.2 1.4 convert_element_type.31
  194.5 0.7 copy-done
  195.2 0.0 copy-start.5
  195.2 2.4 %copy.22 = f32[256,2,768]{2,1,0:T(2,128)} copy(f32[256,2,768]{2,0,1:T(8,128)S(1)} %bitcast.31) | data formatting | bytes 3145728
  197.6 0.0 copy-start.6
  197.6 0.0 copy-start.8
  197.6 0.0 copy-start.7
  197.6 0.0 copy-done.5
  197.6 1.7 copy.21
  199.3 0.0 copy-done.6
  199.3 0.9 bitcast_convert_fusion.3
  200.2 0.0 copy-done.8
  200.2 0.6 reduce
  200.8 0.0 copy-done.7
  200.8 0.6 reduce.1
  (2 shorter events, 0.0 us)
Async XLA Ops:
  0.6 2.5 %copy-start.3 = (bf16[256,2,768]{2,1,0:T(2,128)(2,1)S(1)}, bf16[256,2,768]{2,1,0:T(2,128)(2,1)}, u32[]{:S(2)}) copy-start(bf16[256,2,768]{2,1,0:T(2,128)(2,1)} %param.19) | copy-start | bytes 2359300
  0.7 3.5 %copy-start.4 = (bf16[256,2,768]{2,1,0:T(2,128)(2,1)S(1)}, bf16[256,2,768]{2,1,0:T(2,128)(2,1)}, u32[]{:S(2)}) copy-start(bf16[256,2,768]{2,1,0:T(2,128)(2,1)} %param.10) | copy-start | bytes 2359300
  3.2 1.9 copy-start.9
  3.2 1.9 copy-start.10
  187.2 4.3 %copy-start.1 = (bf16[4,2,2,2,32,512]{5,4,3,2,1,0:T(8,128)(2,1)S(1)}, bf16[4,2,2,2,32,512]{5,4,3,2,1,0:T(8,128)(2,1)}, u32[]{:S(2)}) copy-start(bf16[4,2,2,2,32,512]{5,4,3,2,1,0:T(8,128)(2,1)} %get-tuple-element.26) | copy-start | bytes 3145732
  191.5 1.7 copy-start.2
  193.2 2.0 %copy-start = (f32[2,256,768]{2,1,0:T(8,128)S(1)}, f32[2,256,768]{2,1,0:T(8,128)}, u32[]{:S(2)}) copy-start(f32[2,256,768]{2,1,0:T(8,128)} %get-tuple-element.19) | copy-start | bytes 4718596
  195.2 2.4 %copy-start.5 = (bf16[2,256,768]{2,1,0:T(8,128)(2,1)S(1)}, bf16[2,256,768]{2,1,0:T(8,128)(2,1)}, u32[]{:S(2)}) copy-start(bf16[2,256,768]{2,1,0:T(8,128)(2,1)} %get-tuple-element.18) | copy-start | bytes 2359300
  197.6 1.7 copy-start.6
  197.6 2.6 %copy-start.8 = (f32[1,768]{1,0:T(1,128)S(1)}, f32[1,768]{1,0:T(1,128)}, u32[]{:S(2)}) copy-start(f32[1,768]{1,0:T(1,128)} %get-tuple-element.20) | copy-start | bytes 9220
  197.6 3.2 %copy-start.7 = (f32[1,768]{1,0:T(1,128)S(1)}, f32[1,768]{1,0:T(1,128)}, u32[]{:S(2)}) copy-start(f32[1,768]{1,0:T(1,128)} %get-tuple-element.23) | copy-start | bytes 9220

commit v4 on v3

--- a/solution.py
+++ b/solution.py
@@ -284,10 +284,9 @@
 
     Wq, Wk, Wv, Wo = W0.at[0, 0], W0.at[0, 1], W0.at[1, 0], W0.at[1, 1]
 
-    def halo_start():
-        for r in range(rows):
-            pl.when(has_right)(lambda: halo_right(r).start())
-            pl.when(has_left)(lambda: halo_left(r).start())
+    def halo_start(r):
+        pl.when(has_right)(lambda: halo_right(r).start())
+        pl.when(has_left)(lambda: halo_left(r).start())
 
     at_end = (z == 0) | (z == T - 1)
 
@@ -301,8 +300,10 @@
 
     @pl.when(at_end)
     def _():
+        halo_start(0)
         z_start(2, 1)
-        halo_start()
+        for r in range(1, rows):
+            halo_start(r)
 
     to_1(1, 0)
     to_1(2, 0)
@@ -311,8 +312,10 @@
 
     @pl.when(inside)
     def _():
+        halo_start(0)
         z_start(2, 1)
-        halo_start()
+        for r in range(1, rows):
+            halo_start(r)
 
     to_2(2, 0)
     to_3(1, 0)

time: 202 us -> 202 us (level)
  no operation moved by 1% of the time
where the time goes in v4:
time: 202 us; the launch traced here: 201 us
  Pallas kernels  182 us (90%)
  other arithmetic  12.5 us (6%)
  local copies, waits for them, and re-layouts  6.7 us (3%)
    pallas_call x1, Pallas kernels, per_device(): pl.pallas_call(functools.partial(kernel, T, bits, T * tile, n_sems), out_...  182 us
    unnamed x26, local copies, waits for them, and re-layouts  6.69 us
    convert_element_type x1, other arithmetic, per_device(): f2.reshape(depth, depth).astype(F32)  4.26 us

profile of v4, /device:TPU:0, one launch (start us, length us, event | category | flops | bytes accessed | tf_op | source)
XLA Modules:
  0.0 201.4 jit_solution(2000794032196417794)
XLA Ops:
  0.6 0.0 copy-start.3
  0.7 0.0 copy-start.4
  0.7 2.5 %pad_maximum_fusion = bf16[4,192,768]{2,1,0:T(8,128)(2,1)} fusion(bf16[1,192,768]{2,1,0:T(8,128)(2,1)} %bitcast.37, bf16[3,192,768]{2,1,0:T(8,128)(2,1)} %bitcast.34), kind=kLoop, calls=%fused_computation | loop fusion | flops 589824 | bytes 2359296 | tf_op jit(solution)/shard_map/concatenate | solution.py:916
  3.2 0.0 copy-done.3
  3.2 0.0 copy-start.9
  3.2 0.0 copy-start.10
  3.2 1.0 copy.25
  4.1 0.0 copy-done.4
  4.1 1.0 copy.26
  5.1 0.0 copy-done.9
  5.1 0.0 copy-done.10
  5.1 0.6 maximum_convert_fusion.gain_ref
  5.7 181.5 %shard_map.169 = (bf16[2,256,768]{2,1,0:T(8,128)(2,1)}, f32[2,256,768]{2,1,0:T(8,128)}, f32[1,768]{1,0:T(1,128)}, f32[1,768]{1,0:T(1,128)}, bf16[3,2,96,768]{3,2...) custom-call(s32[2]{0:T(128)} %len_ref.1, ...), custom_call_target="tpu_custom_call" | custom-call | tf_op jit(solution)/shard_map/pallas_call | solution.py:962
  187.2 0.0 copy-start.1
  187.2 4.3 %bitcast_convert_fusion = (f32[768,768]{1,0:T(8,128)}, f32[768,768]{1,0:T(8,128)}) fusion(bf16[2,2,2,96,768]{4,3,2,1,0:T(8,128)(2,1)} %get-tuple-element.25, bf16[2,2,2,96,768]{4,3,2,1,0:T(8,128)(2,1)} %get-tuple-element.24), kind=kLoop, calls=%fused_computation.1 | loop fusion | flops 1179648 | bytes 7077888 | tf_op jit(solution)/shard_map/convert_element_type | solution.py:1000
  191.5 0.0 copy-done.1
  191.5 0.0 copy-start.2
  191.5 1.7 bitcast_convert_fusion.2
  193.2 0.0 copy-start
  193.2 0.0 copy-done.2
  193.2 1.4 convert_element_type.31
  194.5 0.7 copy-done
  195.2 0.0 copy-start.5
  195.2 2.4 %copy.22 = f32[256,2,768]{2,1,0:T(2,128)} copy(f32[256,2,768]{2,0,1:T(8,128)S(1)} %bitcast.31) | data formatting | bytes 3145728
  197.6 0.0 copy-start.6
  197.6 0.0 copy-start.8
  197.6 0.0 copy-start.7
  197.6 0.0 copy-done.5
  197.6 1.7 copy.21
  199.3 0.0 copy-done.6
  199.3 0.9 bitcast_convert_fusion.3
  200.2 0.0 copy-done.8
  200.2 0.6 reduce
  200.8 0.0 copy-done.7
  200.8 0.6 reduce.1
  (2 shorter events, 0.0 us)
Async XLA Ops:
  0.6 2.5 %copy-start.3 = (bf16[256,2,768]{2,1,0:T(2,128)(2,1)S(1)}, bf16[256,2,768]{2,1,0:T(2,128)(2,1)}, u32[]{:S(2)}) copy-start(bf16[256,2,768]{2,1,0:T(2,128)(2,1)} %param.19) | copy-start | bytes 2359300
  0.7 3.5 %copy-start.4 = (bf16[256,2,768]{2,1,0:T(2,128)(2,1)S(1)}, bf16[256,2,768]{2,1,0:T(2,128)(2,1)}, u32[]{:S(2)}) copy-start(bf16[256,2,768]{2,1,0:T(2,128)(2,1)} %param.10) | copy-start | bytes 2359300
  3.2 1.9 copy-start.9
  3.2 1.9 copy-start.10
  187.2 4.3 %copy-start.1 = (bf16[4,2,2,2,32,512]{5,4,3,2,1,0:T(8,128)(2,1)S(1)}, bf16[4,2,2,2,32,512]{5,4,3,2,1,0:T(8,128)(2,1)}, u32[]{:S(2)}) copy-start(bf16[4,2,2,2,32,512]{5,4,3,2,1,0:T(8,128)(2,1)} %get-tuple-element.26) | copy-start | bytes 3145732
  191.5 1.7 copy-start.2
  193.2 2.0 %copy-start = (f32[2,256,768]{2,1,0:T(8,128)S(1)}, f32[2,256,768]{2,1,0:T(8,128)}, u32[]{:S(2)}) copy-start(f32[2,256,768]{2,1,0:T(8,128)} %get-tuple-element.19) | copy-start | bytes 4718596
  195.2 2.4 %copy-start.5 = (bf16[2,256,768]{2,1,0:T(8,128)(2,1)S(1)}, bf16[2,256,768]{2,1,0:T(8,128)(2,1)}, u32[]{:S(2)}) copy-start(bf16[2,256,768]{2,1,0:T(8,128)(2,1)} %get-tuple-element.18) | copy-start | bytes 2359300
  197.6 1.7 copy-start.6
  197.6 2.6 %copy-start.8 = (f32[1,768]{1,0:T(1,128)S(1)}, f32[1,768]{1,0:T(1,128)}, u32[]{:S(2)}) copy-start(f32[1,768]{1,0:T(1,128)} %get-tuple-element.20) | copy-start | bytes 9220
  197.6 3.2 %copy-start.7 = (f32[1,768]{1,0:T(1,128)S(1)}, f32[1,768]{1,0:T(1,128)}, u32[]{:S(2)}) copy-start(f32[1,768]{1,0:T(1,128)} %get-tuple-element.23) | copy-start | bytes 9220
